TPU v7x, 32 devices: a whole 2x2x4 slice. The times are simulated.
32 devices in a mesh: dp: 8 (over z, y), mp: 4 (over x, core).
Axes of the slice: x: 2, y: 2, z: 4, core: 2. Of those that a mesh axis runs over, the one named last changes fastest.
Arguments:
- queries: bfloat16 [1024, 2048], P('dp', 'mp'), may hold values from -400 to 400
- encodings: bfloat16 [1024, 896], P('dp'), may hold values from -6 to 6
- kv_weight: bfloat16 [896, 2, 2048], P('dp', None, 'mp'), may hold values from -0.1875 to 0.1875
- pair_list: int32 [16, 2], P('dp'), may hold values from 0 to 7, as said below
- cotangent: bfloat16 [1024, 2048], P('dp', 'mp'), may hold values from -6 to 6
Outputs:
- attended: bfloat16 [1024, 2048], P('dp', 'mp')
- query_grad: bfloat16 [1024, 2048], P('dp', 'mp')
- encoding_grad: bfloat16 [1024, 896], P('dp', 'mp')
- weight_grad: float32 [896, 2, 2048], P('dp', None, 'mp')
Inputs may be any that keep to these rules, and one draw needn't show every extreme that they name: Each dp device owns one neighbour block, block n belongs to dp device n, and pair_list[c, j] is at most 2 positions away from c // 2 along dp, counted around the cycle of 8 devices.
All inputs are finite; a program needn't handle non-finite values.
Results may differ from a plain program's by a relative error of at most 0.034.
The roundings to bfloat16 on the way count: a program that leaves them out, or rounds other values in their place, can miss the bound.
Values may be sent and summed in bfloat16 or wider, within the bound.
A program may use at most 64 MiB of HBM per device.

v0:
```python
import jax
import jax.numpy as jnp
from jax import lax
from jax.sharding import PartitionSpec as P

HD = 128
SPAN = 64
NROWS = 128
NBR = 2
REACH = 2


def shifted(value, axis, steps):
    count = lax.axis_size(axis)
    pairs = [(source, (source + steps) % count) for source in range(count)]
    return lax.ppermute(value, axis, pairs)


def project(rows, weights):
    return jnp.einsum("re,etx->rtx", rows, weights, preferred_element_type=jnp.float32).astype(
        jnp.bfloat16
    )


def fetch_window(block, reach):
    pieces = []
    for offset in range(-reach, reach + 1):
        if offset == 0:
            pieces.append(block)
        else:
            pieces.append(shifted(block, "dp", -offset))
    return pieces


def return_grads(contrib, reach):
    total = contrib[reach]
    for offset in range(-reach, reach + 1):
        if offset != 0:
            total = total + shifted(contrib[offset + reach], "dp", offset)
    return total


def per_device(queries, encodings, kv_weight, pair_list, cotangent):
    reach = REACH
    device_count = lax.axis_size("dp")
    my_index = lax.axis_index("dp")
    factor = 1.0 / HD**0.5
    weights = lax.all_gather(kv_weight, "dp", axis=0, tiled=True)
    columns = weights.shape[2]
    heads_here = columns // HD
    owned_rows = encodings.shape[0]
    slot_count = owned_rows // NROWS
    window_size = 2 * reach + 1
    own_blocks = project(encodings, weights)
    window = jnp.stack(fetch_window(own_blocks, reach), axis=0)
    pair_ids = pair_list.reshape(-1)
    owners = pair_ids // slot_count
    slot_index = pair_ids % slot_count
    offsets = (owners - my_index + reach) % device_count
    window_index = offsets * slot_count + slot_index
    span_count = pair_list.shape[0]
    chosen = jnp.take(window, window_index, axis=0).reshape(
        span_count, NBR * NROWS, 2, heads_here, HD
    )
    keys = chosen[:, :, 0]
    values = chosen[:, :, 1]
    query_rows = queries.reshape(span_count, SPAN, heads_here, HD)
    grad_rows = cotangent.reshape(span_count, SPAN, heads_here, HD)
    scores = (
        jnp.einsum("cqhd,ckhd->chqk", query_rows, keys, preferred_element_type=jnp.float32) * factor
    )
    probs = jax.nn.softmax(scores, axis=-1)
    probs_b = probs.astype(jnp.bfloat16)
    attended = jnp.einsum(
        "chqk,ckhd->cqhd", probs_b, values, preferred_element_type=jnp.float32
    ).astype(jnp.bfloat16)
    dprobs = jnp.einsum("cqhd,ckhd->chqk", grad_rows, values, preferred_element_type=jnp.float32)
    delta = jnp.sum(probs * dprobs, axis=-1, keepdims=True)
    dscores = (probs * (dprobs - delta) * factor).astype(jnp.bfloat16)
    query_grad = jnp.einsum(
        "chqk,ckhd->cqhd", dscores, keys, preferred_element_type=jnp.float32
    ).astype(jnp.bfloat16)
    key_grad = jnp.einsum(
        "chqk,cqhd->ckhd", dscores, query_rows, preferred_element_type=jnp.float32
    )
    value_grad = jnp.einsum(
        "chqk,cqhd->ckhd", probs_b, grad_rows, preferred_element_type=jnp.float32
    )
    pair_grads = jnp.stack([key_grad, value_grad], axis=2).reshape(
        span_count * NBR, NROWS * 2 * columns
    )
    one_hot = (
        window_index[:, None] == jnp.arange(window_size * slot_count, dtype=jnp.int32)[None, :]
    ).astype(jnp.float32)
    contrib = jnp.einsum("pw,pr->wr", one_hot, pair_grads, precision=lax.Precision.HIGHEST)
    contrib = contrib.reshape(window_size, owned_rows, 2, columns)
    block_grad = return_grads([contrib[index] for index in range(window_size)], reach)
    block_grad_b = block_grad.astype(jnp.bfloat16)
    partial_sum = jnp.einsum(
        "rtx,etx->re", block_grad_b, weights, preferred_element_type=jnp.float32
    )
    encoding_grad = lax.psum_scatter(
        partial_sum.astype(jnp.bfloat16), "mp", scatter_dimension=1, tiled=True
    )
    flat_grad = block_grad_b.reshape(owned_rows, 2 * columns)
    product = jnp.einsum("rc,rx->cx", encodings, flat_grad, preferred_element_type=jnp.float32)
    weight_grad = lax.psum_scatter(
        product.reshape(kv_weight.shape[0] * lax.axis_size("dp"), 2, columns),
        "dp",
        scatter_dimension=0,
        tiled=True,
    )
    return (
        attended.reshape(span_count * SPAN, columns),
        query_grad.reshape(span_count * SPAN, columns),
        encoding_grad,
        weight_grad,
    )


def solution(mesh):
    return jax.shard_map(
        per_device,
        mesh=mesh,
        in_specs=(P("dp", "mp"), P("dp", None), P("dp", None, "mp"), P("dp", None), P("dp", "mp")),
        out_specs=(P("dp", "mp"), P("dp", "mp"), P("dp", "mp"), P("dp", None, "mp")),
        check_vma=False,
    )
```

profile of v0, /device:TPU:0, one launch (start us, length us, event | category | flops | bytes accessed | tf_op | source)
XLA Modules:
  0.0 335.5 jit_solution(6586403726418409633)
XLA Ops:
  7.2 1.8 copy.37
  10.0 49.8 %all-gather.2.cloned.1.call-done = bf16[896,2,512]{2,0,1:T(8,128)(2,1)} async-done(((bf16[112,2,512]{2,0,1:T(8,128)(2,1)}), bf16[896,2,512]{2,0,1:T(8,128)(2,1)}) %all-gather.2.cloned.1.call-update) | async-done | bytes 1835024 | tf_op jit(solution)/shard_map/all_gather | solution.py:48
  59.8 1.9 convolution_convert_fusion
  61.7 2.1 collective-permute-start
  65.2 4.2 %collective-permute-start.2 = (bf16[128,2,512]{2,0,1:T(8,128)(2,1)S(1)}, bf16[128,2,512]{2,0,1:T(8,128)(2,1)S(1)}, u32[]{:S(2)}, u32[]{:S(2)}) collective-permute-start(bf16[128,2,512]{2,0,1:T(8,128)(2,1)S(1)} %convolution_convert_fusion), channel_id=1, source_target_pairs={{0,28},{4,0},{8,4},{12,8},{16,12},{20,16},{24,20},{28,24},{1,29},{... | collective-permute-start | bytes 786440 | tf_op jit(solution)/shard_map/ppermute | solution.py:16
  69.4 3.4 %collective-permute-done = bf16[128,2,512]{2,0,1:T(8,128)(2,1)S(1)} collective-permute-done((bf16[128,2,512]{2,0,1:T(8,128)(2,1)S(1)}, bf16[128,2,512]{2,0,1:T(8,128)(2,1)S(1)}, u32[]{:S(2)}, u32[]{:S(2)}) %collective-permute-start) | collective-permute-done | bytes 262176 | tf_op jit(solution)/shard_map/ppermute | solution.py:16
  72.9 5.6 %collective-permute-done.1 = bf16[128,2,512]{2,0,1:T(8,128)(2,1)S(1)} collective-permute-done((bf16[128,2,512]{2,0,1:T(8,128)(2,1)S(1)}, bf16[128,2,512]{2,0,1:T(8,128)(2,1)S(1)}, u32[]{:S(2)}, u32[]{:S(2)}) %collective-permute-start.1) | collective-permute-done | bytes 262176 | tf_op jit(solution)/shard_map/ppermute | solution.py:16
  78.6 3.3 collective-permute-done.3
  87.5 5.7 %convolution_bitcast_fusion.1 = f32[2,256,1,4,128]{4,1,3,0,2:T(8,128)} fusion(f32[2,4,64,256]{3,2,1,0:T(8,128)} %convolution_bitcast_fusion.2, bf16[2,64,4,128]{3,2,1,0:T(4,128)(2,1)S(1)} %reshape.123, f32[2,4,64,256]{3,2,1,0:T(8,128)} %get-tuple-element.12, f32[2,4,64]{2,1,0:T(4,128)S(1)} %get-tuple-element.11), kind=kOutput, calls=%fused_computation.5 | convolution fusion | flops 34472704 | bytes 2230272 | tf_op jit(solution)/shard_map/chqk,cqhd->ckhd/dot_general | solution.py:83
  93.1 1.4 pad_maximum_fusion
  94.5 2.7 copy.46
  97.2 3.0 reshape.127
  100.2 2.8 fusion.25
  103.0 10.1 %slice_reduce_fusion.3 = (f32[131072]{0:T(1024)S(1)}, f32[131072]{0:T(1024)}, f32[131072]{0:T(1024)S(1)}, f32[131072]{0:T(1024)S(1)}, f32[131072]{0:T(1024)S(1)}) fusion(f32[5,131072]{1,0:T(8,128)S(1)} %fusion.25), kind=kLoop, calls=%fused_computation.29 | loop fusion | bytes 5242880 | tf_op jit(solution)/shard_map/slice | solution.py:97
  113.1 2.1 squeeze.27
  115.2 2.1 copy.51
  118.9 2.1 copy.50
  122.8 4.2 %collective-permute-start.5 = (f32[128,2,512]{0,2,1:T(8,128)}, f32[128,2,512]{0,2,1:T(8,128)}, u32[]{:S(2)}, u32[]{:S(2)}) collective-permute-start(f32[128,2,512]{0,2,1:T(8,128)} %copy.49), channel_id=1, source_target_pairs={{0,28},{4,0},{8,4},{12,8},{16,12},{20,16},{24,20},{28,24},{1,29},{... | collective-permute-start | bytes 1572872 | tf_op jit(solution)/shard_map/ppermute | solution.py:16
  127.5 1.5 collective-permute-start.4
  129.5 4.8 %collective-permute-done.7 = f32[128,2,512]{0,2,1:T(8,128)} collective-permute-done((f32[128,2,512]{0,2,1:T(8,128)}, f32[128,2,512]{0,2,1:T(8,128)}, u32[]{:S(2)}, u32[]{:S(2)}) %collective-permute-start.7) | collective-permute-done | bytes 524320 | tf_op jit(solution)/shard_map/ppermute | solution.py:16
  134.3 11.2 %collective-permute-done.6 = f32[128,2,512]{0,2,1:T(8,128)} collective-permute-done((f32[128,2,512]{0,2,1:T(8,128)}, f32[128,2,512]{0,2,1:T(8,128)}, u32[]{:S(2)}, u32[]{:S(2)}) %collective-permute-start.6) | collective-permute-done | bytes 524320 | tf_op jit(solution)/shard_map/ppermute | solution.py:16
  145.5 2.2 collective-permute-done.5
  147.7 7.3 %collective-permute-done.4 = f32[128,2,512]{0,2,1:T(8,128)} collective-permute-done((f32[128,2,512]{0,2,1:T(8,128)S(1)}, f32[128,2,512]{0,2,1:T(8,128)}, u32[]{:S(2)}, u32[]{:S(2)}) %collective-permute-start.4) | collective-permute-done | bytes 524320 | tf_op jit(solution)/shard_map/ppermute | solution.py:16
  155.0 1.6 add_convert_fusion
  156.6 2.5 fusion.36
  159.1 6.6 %copy.53 = f32[896,2,512]{2,1,0:T(2,128)} copy(f32[896,2,512]{0,2,1:T(8,128)} %bitcast.74) | data formatting | bytes 7340032 | tf_op jit(solution)/shard_map/reshape | solution.py:108
  167.6 4.0 %fusion.11 = bf16[2,64,4,128]{3,1,2,0:T(8,128)(2,1)S(1)} fusion(f32[2,4,64,256]{3,2,1,0:T(8,128)} %convolution_bitcast_fusion.2, bf16[2,256,2,4,128]{4,1,3,0,2:T(8,128)(2,1)S(1)} %copy_select_fusion, f32[2,4,64,256]{3,2,1,0:T(8,128)} %get-tuple-element.12, f32[2,4,64]{2,1,0:T(4,128)S(1)} %get-tuple-element.11), kind=kOutput, calls=%fused_computation.21 | convolution fusion | flops 34538240 | bytes 2760704 | tf_op jit(solution)/shard_map/chqk,ckhd->cqhd/dot_general | solution.py:80
  171.6 1.3 fusion.9
  173.0 2.2 fusion.10
  176.1 130.9 %all-reduce.3.cloned.1.call-done = f32[896,2,512]{2,1,0:T(2,128)} async-done(((f32[896,2,512]{2,1,0:T(2,128)}), f32[896,2,512]{2,1,0:T(2,128)}) %all-reduce.3.cloned.1.call-update) | async-done | bytes 3670032
  307.0 1.8 constant_dynamic-slice_fusion
  308.8 20.1 %reduce-scatter.2.cloned.1.call-done = bf16[128,224]{0,1:T(8,128)(2,1)} async-done(((bf16[128,896]{0,1:T(8,128)(2,1)}), bf16[128,224]{0,1:T(8,128)(2,1)}) %reduce-scatter.2.cloned.1.call-update) | async-done | bytes 57360 | tf_op jit(solution)/shard_map/reduce_scatter | solution.py:102
  (59 shorter events, 14.7 us)
Async XLA Ops:
  7.2 52.6 %copy-start = (bf16[128,896]{1,0:T(8,128)(2,1)S(1)}, bf16[128,896]{1,0:T(8,128)(2,1)}, u32[]{:S(2)}) copy-start(bf16[128,896]{1,0:T(8,128)(2,1)} %param.6) | copy-start | bytes 688132
  7.2 57.3 %copy-start.4 = (bf16[128,512]{1,0:T(8,128)(2,1)S(1)}, bf16[128,512]{1,0:T(8,128)(2,1)}, u32[]{:S(2)}) copy-start(bf16[128,512]{1,0:T(8,128)(2,1)} %param.9) | copy-start | bytes 393220
  7.2 57.9 %copy-start.5 = (bf16[128,512]{1,0:T(8,128)(2,1)S(1)}, bf16[128,512]{1,0:T(8,128)(2,1)}, u32[]{:S(2)}) copy-start(bf16[128,512]{1,0:T(8,128)(2,1)} %param.5) | copy-start | bytes 393220
  7.2 52.6 %all-gather.2.cloned.1.call-start = ((), (), s32[]{:S(2)}) async-start(), calls=%async_computation.1 | async-start | bytes 2064384 | tf_op jit(solution)/shard_map/all_gather | solution.py:48
  9.0 297.9 %all-reduce.3.cloned.1.call-start = ((), (), s32[]{:S(2)}) async-start(), calls=%async_computation.3 | async-start | bytes 7340032
  61.7 11.1 %collective-permute-start = (bf16[128,2,512]{2,0,1:T(8,128)(2,1)S(1)}, bf16[128,2,512]{2,0,1:T(8,128)(2,1)S(1)}, u32[]{:S(2)}, u32[]{:S(2)}) collective-permute-start(bf16[128,2,512]{2,0,1:T(8,128)(2,1)S(1)} %convolution_convert_fusion), channel_id=1, source_target_pairs={{0,8},{4,12},{8,16},{12,20},{16,24},{20,28},{24,0},{28,4},{1,9},{5... | collective-permute-start | bytes 786440 | tf_op jit(solution)/shard_map/ppermute | solution.py:16
  63.9 14.6 %collective-permute-start.1 = (bf16[128,2,512]{2,0,1:T(8,128)(2,1)S(1)}, bf16[128,2,512]{2,0,1:T(8,128)(2,1)S(1)}, u32[]{:S(2)}, u32[]{:S(2)}) collective-permute-start(bf16[128,2,512]{2,0,1:T(8,128)(2,1)S(1)} %convolution_convert_fusion), channel_id=1, source_target_pairs={{0,4},{4,8},{8,12},{12,16},{16,20},{20,24},{24,28},{28,0},{1,5},{5... | collective-permute-start | bytes 786440 | tf_op jit(solution)/shard_map/ppermute | solution.py:16
  65.2 13.4 %collective-permute-start.2 = (bf16[128,2,512]{2,0,1:T(8,128)(2,1)S(1)}, bf16[128,2,512]{2,0,1:T(8,128)(2,1)S(1)}, u32[]{:S(2)}, u32[]{:S(2)}) collective-permute-start(bf16[128,2,512]{2,0,1:T(8,128)(2,1)S(1)} %convolution_convert_fusion), channel_id=1, source_target_pairs={{0,28},{4,0},{8,4},{12,8},{16,12},{20,16},{24,20},{28,24},{1,29},{... | collective-permute-start | bytes 786440 | tf_op jit(solution)/shard_map/ppermute | solution.py:16
  69.4 12.4 %collective-permute-start.3 = (bf16[128,2,512]{2,0,1:T(8,128)(2,1)S(1)}, bf16[128,2,512]{2,0,1:T(8,128)(2,1)S(1)}, u32[]{:S(2)}, u32[]{:S(2)}) collective-permute-start(bf16[128,2,512]{2,0,1:T(8,128)(2,1)S(1)} %convolution_convert_fusion), channel_id=1, source_target_pairs={{0,24},{4,28},{8,0},{12,4},{16,8},{20,12},{24,16},{28,20},{1,25},{... | collective-permute-start | bytes 786440 | tf_op jit(solution)/shard_map/ppermute | solution.py:16
  82.9 0.9 copy-start.3
  85.2 7.9 %copy-start.2 = (f32[2,4,64,256]{3,2,1,0:T(8,128)}, f32[2,4,64,256]{3,2,1,0:T(8,128)S(1)}, u32[]{:S(2)}) copy-start(f32[2,4,64,256]{3,2,1,0:T(8,128)S(1)} %fusion.7) | copy-start | bytes 1572868
  117.3 17.0 %collective-permute-start.7 = (f32[128,2,512]{0,2,1:T(8,128)}, f32[128,2,512]{0,2,1:T(8,128)}, u32[]{:S(2)}, u32[]{:S(2)}) collective-permute-start(f32[128,2,512]{0,2,1:T(8,128)} %copy.51), channel_id=1, source_target_pairs={{0,8},{4,12},{8,16},{12,20},{16,24},{20,28},{24,0},{28,4},{1,9},{5... | collective-permute-start | bytes 1572872 | tf_op jit(solution)/shard_map/ppermute | solution.py:16
  121.0 24.5 %collective-permute-start.6 = (f32[128,2,512]{0,2,1:T(8,128)}, f32[128,2,512]{0,2,1:T(8,128)}, u32[]{:S(2)}, u32[]{:S(2)}) collective-permute-start(f32[128,2,512]{0,2,1:T(8,128)} %copy.50), channel_id=1, source_target_pairs={{0,4},{4,8},{8,12},{12,16},{16,20},{20,24},{24,28},{28,0},{1,5},{5... | collective-permute-start | bytes 1572872 | tf_op jit(solution)/shard_map/ppermute | solution.py:16
  122.8 24.8 %collective-permute-start.5 = (f32[128,2,512]{0,2,1:T(8,128)}, f32[128,2,512]{0,2,1:T(8,128)}, u32[]{:S(2)}, u32[]{:S(2)}) collective-permute-start(f32[128,2,512]{0,2,1:T(8,128)} %copy.49), channel_id=1, source_target_pairs={{0,28},{4,0},{8,4},{12,8},{16,12},{20,16},{24,20},{28,24},{1,29},{... | collective-permute-start | bytes 1572872 | tf_op jit(solution)/shard_map/ppermute | solution.py:16
  127.5 27.5 %collective-permute-start.4 = (f32[128,2,512]{0,2,1:T(8,128)S(1)}, f32[128,2,512]{0,2,1:T(8,128)}, u32[]{:S(2)}, u32[]{:S(2)}) collective-permute-start(f32[128,2,512]{0,2,1:T(8,128)S(1)} %copy.47), channel_id=1, source_target_pairs={{0,24},{4,28},{8,0},{12,4},{16,8},{20,12},{24,16},{28,20},{1,25},{... | collective-permute-start | bytes 1572872 | tf_op jit(solution)/shard_map/ppermute | solution.py:16
  165.7 0.7 copy-start.6
  165.7 5.9 %copy-start.1 = (bf16[896,2,512]{2,0,1:T(8,128)(2,1)S(1)}, bf16[896,2,512]{2,0,1:T(8,128)(2,1)}, u32[]{:S(2)}) copy-start(bf16[896,2,512]{2,0,1:T(8,128)(2,1)} %all-gather.2.cloned.1.call-done) | copy-start | bytes 5505028
  165.7 163.2 %reduce-scatter.2.cloned.1.call-start = ((), (), s32[]{:S(2)}) async-start(), calls=%async_computation.2 | async-start | bytes 286720 | tf_op jit(solution)/shard_map/reduce_scatter | solution.py:102
Sparse Core Ops, SparseCore 0:
  10.8 48.9 all-gather.1
  165.8 141.1 all-reduce.2
  310.0 18.8 reduce-scatter.1
where the time goes:
time: 336 us; the launch traced here: 335 us
  waiting for transfers between devices  239 us (71%)
  local copies, waits for them, and re-layouts  40.4 us (12%)
  matrix products  23.1 us (7%)
  between operations  14.6 us (4%)
  starting transfers between devices  13.8 us (4%)
  other arithmetic  4.91 us (1%)
    unnamed x4, waiting for transfers between devices  131 us
    all_gather x1, waiting for transfers between devices, per_device(): weights = lax.all_gather(kv_weight, 'dp', axis=0, tiled=True)  49.8 us
    ppermute x8, waiting for transfers between devices, shifted(): return lax.ppermute(value, axis, pairs)  37.8 us
    reduce_scatter x1, waiting for transfers between devices, per_device(): lax.psum_scatter(partial_sum.astype(jnp.bfloat16), 'mp', scatter_dimensio...  20.1 us
    ppermute x8, starting transfers between devices, shifted(): return lax.ppermute(value, axis, pairs)  13.7 us
    slice x1, local copies, waits for them, and re-layouts, per_device(): contrib[index]  10.1 us
    squeeze x10, local copies, waits for them, and re-layouts, per_device(): contrib[index]  9.56 us
  transfers between devices with their start and end apart: 11, of which 10 were waited for; matrix products, arithmetic and copies ran while one was open for 5% of the time, Pallas kernels for 0%

commit v1 on v0

--- a/solution.py
+++ b/solution.py
@@ -1,6 +1,10 @@
+import functools
+
 import jax
 import jax.numpy as jnp
 from jax import lax
+from jax.experimental import pallas as pl
+from jax.experimental.pallas import tpu as pltpu
 from jax.sharding import PartitionSpec as P
 
 HD = 128
@@ -8,6 +12,309 @@
 NROWS = 128
 NBR = 2
 REACH = 2
+GATHER_LIMIT = 8
+VMEM_BYTES = 56 * 1024 * 1024
+MESH = pl.DeviceIdType.MESH
+
+
+def gather_kernel(
+    n, m, w_ref, e_ref, q_ref, c_ref, p_ref, w_all, e_all, q_all, c_all, p_all,
+    send_sems, recv_sems, share_send, share_recv, own_sems,
+):
+    me = lax.axis_index("dp")
+    mp = lax.axis_index("mp")
+    half = n // 2
+    depth = me // 2
+    side = me % 2
+    ring = depth + side * (n - 1 - 2 * depth)
+    part = e_ref.shape[0] // m
+
+    def at(position):
+        position = (position + 2 * n) % n
+        upper = position // half
+        return (1 - upper) * 2 * position + upper * (2 * (n - 1 - position) + 1)
+
+    targets = (at(ring + 1), at(ring - 1))
+    barrier = pltpu.get_barrier_semaphore()
+    for target in targets:
+        pl.semaphore_signal(barrier, inc=1, device_id=(target, mp), device_id_type=MESH)
+    for k in range(1, m):
+        pl.semaphore_signal(barrier, inc=1, device_id=(me, (mp + k) % m), device_id_type=MESH)
+    pl.semaphore_wait(barrier, m + 1)
+
+    own_rows = pl.ds(mp * part, part)
+    sources = (w_ref, e_ref.at[own_rows], p_ref, q_ref, c_ref)
+
+    def view(a, slot):
+        if a == 1:
+            return e_all.at[slot, own_rows]
+        return (w_all, None, p_all, q_all, c_all)[a].at[slot]
+
+    def travels(d, step, a):
+        if step < half:
+            return True
+        return step == half and (a < 3) == (d == 0)
+
+    def slot_of(d, step):
+        return at(ring - step) if d == 0 else at(ring + step)
+
+    def send(d, step, a):
+        slot = slot_of(d, step - 1)
+        return pltpu.make_async_remote_copy(
+            src_ref=sources[a] if step == 1 else view(a, slot),
+            dst_ref=view(a, slot),
+            send_sem=send_sems.at[d, step - 1, a],
+            recv_sem=recv_sems.at[d, step - 1, a],
+            device_id=(targets[d], mp),
+            device_id_type=MESH,
+        )
+
+    def arrival(d, step, a):
+        slot = slot_of(d, step)
+        return pltpu.make_async_remote_copy(
+            src_ref=view(a, slot),
+            dst_ref=view(a, slot),
+            send_sem=send_sems.at[d, step - 1, a],
+            recv_sem=recv_sems.at[d, step - 1, a],
+            device_id=(targets[d], mp),
+            device_id_type=MESH,
+        )
+
+    def share(d, step, k, arriving):
+        slot = slot_of(d, step)
+        row = (mp + m - k) % m if arriving else mp
+        block = e_all.at[slot, pl.ds(row * part, part)]
+        return pltpu.make_async_remote_copy(
+            src_ref=block,
+            dst_ref=block,
+            send_sem=share_send.at[d, step - 1, k - 1],
+            recv_sem=share_recv.at[d, step - 1, k - 1],
+            device_id=(me, (mp + k) % m),
+            device_id_type=MESH,
+        )
+
+    sent = []
+    shared = []
+    for a in range(5):
+        for d in range(2):
+            copy = send(d, 1, a)
+            copy.start()
+            sent.append(copy)
+    own = [
+        pltpu.make_async_copy(source, whole.at[me], own_sems.at[i])
+        for i, (source, whole) in enumerate(
+            ((w_ref, w_all), (e_ref, e_all), (p_ref, p_all), (q_ref, q_all), (c_ref, c_all))
+        )
+    ]
+    for copy in own:
+        copy.start()
+    for step in range(1, half + 1):
+        for a in range(5):
+            for d in range(2):
+                if not travels(d, step, a):
+                    continue
+                arrival(d, step, a).wait_recv()
+                if travels(d, step + 1, a):
+                    copy = send(d, step + 1, a)
+                    copy.start()
+                    sent.append(copy)
+                if a == 1:
+                    for k in range(1, m):
+                        copy = share(d, step, k, False)
+                        copy.start()
+                        shared.append((copy, d, step, k))
+    for copy, d, step, k in shared:
+        share(d, step, k, True).wait_recv()
+    for copy, d, step, k in shared:
+        copy.wait_send()
+    for copy in sent:
+        copy.wait_send()
+    for copy in own:
+        copy.wait()
+
+
+def gather(n, m, w, e, q, c, p):
+    half = n // 2
+    arrays = (w, e, p, q, c)
+    any_spec = pl.BlockSpec(memory_space=pl.ANY)
+    return pl.pallas_call(
+        functools.partial(gather_kernel, n, m),
+        out_shape=[jax.ShapeDtypeStruct((n,) + x.shape, x.dtype) for x in (w, e, q, c, p)],
+        in_specs=[any_spec] * 5,
+        out_specs=[any_spec] * 5,
+        scratch_shapes=[
+            pltpu.SemaphoreType.DMA((2, half, 5)),
+            pltpu.SemaphoreType.DMA((2, half, 5)),
+            pltpu.SemaphoreType.DMA((2, half, m - 1)),
+            pltpu.SemaphoreType.DMA((2, half, m - 1)),
+            pltpu.SemaphoreType.DMA((5,)),
+        ],
+        compiler_params=pltpu.CompilerParams(collective_id=0, has_side_effects=True),
+        name="gather_inputs",
+    )(w, e, q, c, p)
+
+
+def dot(a, b, da, db):
+    return lax.dot_general(a, b, (((da,), (db,)), ((), ())), preferred_element_type=jnp.float32)
+
+
+def local_kernel(
+    n, m, p_ref, w_ref, e_ref, q_ref, c_ref, att_ref, qg_ref, part_ref, wg_ref, proj, grads, grads_b
+):
+    me = lax.axis_index("dp")
+    width = q_ref.shape[1]
+    heads = width // HD
+    rows_dev = e_ref.shape[0] // n
+    spans_dev = q_ref.shape[0] // n // SPAN
+    factor = 1.0 / HD**0.5
+
+    @pl.loop(0, n)
+    def _(block):
+        proj[block] = dot(
+            e_ref[pl.ds(block * rows_dev, rows_dev), :], w_ref[...], 1, 0
+        ).astype(jnp.bfloat16)
+        grads[block] = jnp.zeros(grads.shape[1:], jnp.float32)
+
+    @pl.loop(0, n * spans_dev)
+    def _(span):
+        owner = span // spans_dev
+        inner = span % spans_dev
+        first = p_ref[owner, 0, inner * NBR]
+        second = p_ref[owner, 0, inner * NBR + 1]
+        rows = pl.ds(span * SPAN, SPAN)
+        for h in range(heads):
+            cols = slice(h * HD, (h + 1) * HD)
+            vcols = slice(width + h * HD, width + (h + 1) * HD)
+            keys = jnp.concatenate([proj[first, :, cols], proj[second, :, cols]], axis=0)
+            values = jnp.concatenate([proj[first, :, vcols], proj[second, :, vcols]], axis=0)
+            query = q_ref[rows, cols]
+            cot = c_ref[rows, cols]
+            scores = dot(query, keys, 1, 1) * factor
+            top = jnp.max(scores, axis=-1, keepdims=True)
+            raised = jnp.exp(scores - top)
+            probs = raised / jnp.sum(raised, axis=-1, keepdims=True)
+            probs_b = probs.astype(jnp.bfloat16)
+            dprobs = dot(cot, values, 1, 1)
+            delta = jnp.sum(probs * dprobs, axis=-1, keepdims=True)
+            dscores = (probs * (dprobs - delta) * factor).astype(jnp.bfloat16)
+            key_grad = dot(dscores, query, 0, 0)
+            value_grad = dot(probs_b, cot, 0, 0)
+            grads[first, :, cols] += key_grad[:NROWS]
+            grads[second, :, cols] += key_grad[NROWS:]
+            grads[first, :, vcols] += value_grad[:NROWS]
+            grads[second, :, vcols] += value_grad[NROWS:]
+
+            @pl.when(owner == me)
+            def _():
+                own = pl.ds(pl.multiple_of(inner * SPAN, SPAN), SPAN)
+                att_ref[own, cols] = dot(probs_b, values, 1, 0).astype(jnp.bfloat16)
+                qg_ref[own, cols] = dot(dscores, keys, 1, 0).astype(jnp.bfloat16)
+
+    @pl.loop(0, n)
+    def _(block):
+        grads_b[pl.ds(block * rows_dev, rows_dev), :] = grads[block].astype(jnp.bfloat16)
+
+    own_grads = grads_b[pl.ds(me * rows_dev, rows_dev), :]
+    partial = dot(own_grads, w_ref[...], 1, 1).astype(jnp.bfloat16)
+    piece = part_ref.shape[2]
+    for k in range(m):
+        part_ref[k] = partial[:, k * piece : (k + 1) * piece]
+    depth, enc = wg_ref.shape[0], e_ref.shape[1]
+    picked = (
+        lax.broadcasted_iota(jnp.int32, (depth, enc), 0) + me * depth
+        == lax.broadcasted_iota(jnp.int32, (depth, enc), 1)
+    ).astype(jnp.bfloat16)
+    columns = dot(picked, e_ref[...], 1, 1).astype(jnp.bfloat16)
+    wg_ref[...] = dot(columns, grads_b[...], 1, 0)
+
+
+def local_part(n, m, p, w, e, q, c):
+    vmem = pl.BlockSpec(memory_space=pltpu.VMEM)
+    depth, width = w.shape[0] // n, q.shape[1]
+    rows, tokens, enc = e.shape[0] // n, q.shape[0] // n, e.shape[1]
+    return pl.pallas_call(
+        functools.partial(local_kernel, n, m),
+        out_shape=[
+            jax.ShapeDtypeStruct((tokens, width), jnp.bfloat16),
+            jax.ShapeDtypeStruct((tokens, width), jnp.bfloat16),
+            jax.ShapeDtypeStruct((m, rows, enc // m), jnp.bfloat16),
+            jax.ShapeDtypeStruct((depth, 2 * width), jnp.float32),
+        ],
+        in_specs=[pl.BlockSpec(memory_space=pltpu.SMEM)] + [vmem] * 4,
+        out_specs=[vmem] * 4,
+        scratch_shapes=[
+            pltpu.VMEM((n, rows, 2 * width), jnp.bfloat16),
+            pltpu.VMEM((n, rows, 2 * width), jnp.float32),
+            pltpu.VMEM((n * rows, 2 * width), jnp.bfloat16),
+        ],
+        compiler_params=pltpu.CompilerParams(vmem_limit_bytes=VMEM_BYTES),
+        name="attention_and_gradients",
+    )(p, w, e, q, c)
+
+
+def group_sum_kernel(m, part_ref, out_ref, landed, send_sems, recv_sems):
+    me = lax.axis_index("dp")
+    mp = lax.axis_index("mp")
+    barrier = pltpu.get_barrier_semaphore()
+    for k in range(1, m):
+        pl.semaphore_signal(barrier, inc=1, device_id=(me, (mp + k) % m), device_id_type=MESH)
+    pl.semaphore_wait(barrier, m - 1)
+    copies = []
+    for k in range(1, m):
+        target = (mp + k) % m
+        copy = pltpu.make_async_remote_copy(
+            src_ref=part_ref.at[target],
+            dst_ref=landed.at[k - 1],
+            send_sem=send_sems.at[k - 1],
+            recv_sem=recv_sems.at[k - 1],
+            device_id=(me, target),
+            device_id_type=MESH,
+        )
+        copy.start()
+        copies.append(copy)
+    total = part_ref[mp].astype(jnp.float32)
+    for k in range(1, m):
+        copies[k - 1].wait_recv()
+        total = total + landed[k - 1].astype(jnp.float32)
+    out_ref[...] = total.astype(out_ref.dtype)
+    for copy in copies:
+        copy.wait_send()
+
+
+def group_sum(m, part):
+    vmem = pl.BlockSpec(memory_space=pltpu.VMEM)
+    return pl.pallas_call(
+        functools.partial(group_sum_kernel, m),
+        out_shape=jax.ShapeDtypeStruct(part.shape[1:], part.dtype),
+        in_specs=[vmem],
+        out_specs=vmem,
+        scratch_shapes=[
+            pltpu.VMEM((m - 1,) + part.shape[1:], part.dtype),
+            pltpu.SemaphoreType.DMA((m - 1,)),
+            pltpu.SemaphoreType.DMA((m - 1,)),
+        ],
+        compiler_params=pltpu.CompilerParams(collective_id=1, has_side_effects=True),
+        name="group_sum",
+    )(part)
+
+
+def per_device_gathered(n, m, queries, encodings, kv_weight, pair_list, cotangent):
+    depth, _, width = kv_weight.shape
+    pairs = jnp.pad(pair_list.reshape(1, -1), ((0, 7), (0, 128 - pair_list.size)))
+    w, e, q, c, p = gather(
+        n, m, kv_weight.reshape(depth, 2 * width), encodings, queries, cotangent, pairs
+    )
+    attended, query_grad, part, weight_grad = local_part(
+        n,
+        m,
+        p,
+        w.reshape(n * depth, 2 * width),
+        e.reshape(-1, e.shape[2]),
+        q.reshape(-1, width),
+        c.reshape(-1, width),
+    )
+    encoding_grad = group_sum(m, part)
+    return attended, query_grad, encoding_grad, weight_grad.reshape(depth, 2, width)
 
 
 def shifted(value, axis, steps):
@@ -119,8 +426,12 @@
 
 
 def solution(mesh):
+    n, m = mesh.shape["dp"], mesh.shape["mp"]
+    body = per_device
+    if n == GATHER_LIMIT:
+        body = functools.partial(per_device_gathered, n, m)
     return jax.shard_map(
-        per_device,
+        body,
         mesh=mesh,
         in_specs=(P("dp", "mp"), P("dp", None), P("dp", None, "mp"), P("dp", None), P("dp", "mp")),
         out_specs=(P("dp", "mp"), P("dp", "mp"), P("dp", "mp"), P("dp", None, "mp")),

time: 336 us -> 118 us (0.35)
  waiting for transfers between devices: 239 us -> 0 us
  Pallas kernels: 0 us -> 110 us
  local copies, waits for them, and re-layouts: 40.4 us -> 6.74 us
  matrix products: 23.1 us -> 0 us
  between operations: 14.6 us -> 0.65 us
  starting transfers between devices: 13.8 us -> 0 us
  other arithmetic: 4.91 us -> 0 us
    unnamed x4 -> x0, waiting for transfers between devices: 131 us -> none
    pallas_call x0 -> x3, Pallas kernels: none -> 110 us  [the longest x1 52.2 us: gather(): pl.pallas_call(functools.partial(gather_kernel, n, m), out_shape=[jax.Sha...]
    all_gather x1 -> x0, waiting for transfers between devices: 49.8 us -> none  [per_device(): weights = lax.all_gather(kv_weight, 'dp', axis=0, tiled=True)]
    ppermute x8 -> x0, waiting for transfers between devices: 37.8 us -> none  [shifted(): return lax.ppermute(value, axis, pairs)]
    dot_general x10 -> x0, matrix products: 23.1 us -> none  [the longest x1 5.67 us: per_device(): jnp.einsum('chqk,cqhd->ckhd', dscores, query_rows, preferred_element_type...]
    reduce_scatter x1 -> x0, waiting for transfers between devices: 20.1 us -> none  [per_device(): lax.psum_scatter(partial_sum.astype(jnp.bfloat16), 'mp', scatter_dimensio...]
    ppermute x8 -> x0, starting transfers between devices: 13.7 us -> none  [shifted(): return lax.ppermute(value, axis, pairs)]
    slice x1 -> x0, local copies, waits for them, and re-layouts: 10.1 us -> none  [per_device(): contrib[index]]
  transfers between devices with their start and end apart: 11 -> 0, of which waited for: 10 -> 0; matrix products, arithmetic and copies ran while one was open for 5% -> 0% of each run, Pallas kernels for 0% -> 0%
where the time goes in v1:
time: 118 us; the launch traced here: 117 us
  Pallas kernels  110 us (93%)
  local copies, waits for them, and re-layouts  6.74 us (6%)
    pallas_call x1, Pallas kernels, gather(): pl.pallas_call(functools.partial(gather_kernel, n, m), out_shape=[jax.Sha...  52.2 us
    pallas_call x1, Pallas kernels, local_part(): pl.pallas_call(functools.partial(local_kernel, n, m), out_shape=[jax.Shap...  50.9 us
    pallas_call x1, Pallas kernels, group_sum(): pl.pallas_call(functools.partial(group_sum_kernel, m), out_shape=jax.Shap...  6.59 us
    unnamed x2, local copies, waits for them, and re-layouts  3.22 us

profile of v1, /device:TPU:0, one launch (start us, length us, event | category | flops | bytes accessed | tf_op | source)
XLA Modules:
  0.0 117.1 jit_solution(1157656599379716546)
XLA Ops:
  0.6 0.8 reshape.30
  1.4 0.6 pad.4.p_ref
  2.0 1.7 %copy.10 = bf16[14,8,2,512]{3,1,2,0:T(8,128)(2,1)} copy(bf16[14,8,2,512]{3,2,1,0:T(2,128)(2,1)} %bitcast.11) | data formatting | bytes 458752
  3.6 52.2 %gather_inputs.1 = (bf16[8,112,1024]{2,1,0:T(8,128)(2,1)}, bf16[8,128,896]{2,1,0:T(8,128)(2,1)}, bf16[8,128,512]{2,1,0:T(8,128)(2,1)}, bf16[8,128,512]{2,1,0:T(8,128)(2,1)}, s32[8,8,128]{2,1,0:T(8,128)}) custom-call(bf16[112,1024]{1,0:T(8,128)(2,1)} %bitcast.10, bf16[128,896]{1,0:T(8,128)(2,1)} %e_ref.1, bf16[128,512]{1,0:T(8,128)(2,1)} %q_ref.1, ...), custom_call_target="tpu_custom_call" | custom-call | tf_op jit(solution)/shard_map/gather_inputs/pallas_call | solution.py:140
  55.9 50.9 %attention_and_gradients.1 = (bf16[128,512]{1,0:T(8,128)(2,1)}, bf16[128,512]{1,0:T(8,128)(2,1)}, bf16[4,128,224]{2,1,0:T(8,128)(2,1)}, f32[112,1024]{1,0:T(8,128)}) custom-call(s32[8,8,128]{2,1,0:T(8,128)} %get-tuple-element.13.p_ref, bf16[896,1024]{1,0:T(8,128)(2,1)} %bitcast.6, bf16[1024,896]{1,0:T(8,128)(2,1)} %bitcast.7, bf16[1024,512]{1,0:T(8,128)(2,1)} %bitcast.8, ...), custom_call_target="tpu_custom_call" | custom-call | tf_op jit(solution)/shard_map/attention_and_gradients/pallas_call | solution.py:235
  106.8 6.6 %group_sum.1 = bf16[128,224]{1,0:T(8,128)(2,1)} custom-call(bf16[4,128,224]{2,1,0:T(8,128)(2,1)} %get-tuple-element.20.part_ref), custom_call_target="tpu_custom_call" | custom-call | tf_op jit(solution)/shard_map/group_sum/pallas_call | solution.py:286
  113.4 1.6 %copy.9 = bf16[128,224]{0,1:T(8,128)(2,1)} copy(bf16[128,224]{1,0:T(8,128)(2,1)} %group_sum.1) | data formatting | bytes 114688
  115.0 2.2 %reshape.35 = f32[112,2,512]{2,1,0:T(2,128)} reshape(f32[112,1024]{1,0:T(8,128)} %get-tuple-element.21) | data formatting | bytes 917504 | tf_op jit(solution)/shard_map/reshape | solution.py:317

commit v2 on v1

--- a/solution.py
+++ b/solution.py
@@ -159,7 +159,8 @@
 
 
 def local_kernel(
-    n, m, p_ref, w_ref, e_ref, q_ref, c_ref, att_ref, qg_ref, part_ref, wg_ref, proj, grads, grads_b
+    n, m, p_ref, w_ref, e_ref, q_ref, c_ref, att_ref, qg_ref, part_ref, wg_ref,
+    proj, grads, grads_b, kept,
 ):
     me = lax.axis_index("dp")
     width = q_ref.shape[1]
@@ -167,12 +168,17 @@
     rows_dev = e_ref.shape[0] // n
     spans_dev = q_ref.shape[0] // n // SPAN
     factor = 1.0 / HD**0.5
+    zeros = jnp.zeros((SPAN, HD), jnp.bfloat16)
 
     @pl.loop(0, n)
     def _(block):
-        proj[block] = dot(
-            e_ref[pl.ds(block * rows_dev, rows_dev), :], w_ref[...], 1, 0
-        ).astype(jnp.bfloat16)
+        rows = dot(e_ref[pl.ds(block * rows_dev, rows_dev), :], w_ref[...], 1, 0)
+        rows = rows.astype(jnp.bfloat16)
+        for h in range(heads):
+            for t in range(2):
+                proj[block, :, (2 * h + t) * HD : (2 * h + t + 1) * HD] = rows[
+                    :, t * width + h * HD : t * width + (h + 1) * HD
+                ]
         grads[block] = jnp.zeros(grads.shape[1:], jnp.float32)
 
     @pl.loop(0, n * spans_dev)
@@ -182,37 +188,59 @@
         first = p_ref[owner, 0, inner * NBR]
         second = p_ref[owner, 0, inner * NBR + 1]
         rows = pl.ds(span * SPAN, SPAN)
+        both = [slice(2 * h * HD, 2 * (h + 1) * HD) for h in range(heads)]
+        sides, products = [], []
         for h in range(heads):
             cols = slice(h * HD, (h + 1) * HD)
-            vcols = slice(width + h * HD, width + (h + 1) * HD)
-            keys = jnp.concatenate([proj[first, :, cols], proj[second, :, cols]], axis=0)
-            values = jnp.concatenate([proj[first, :, vcols], proj[second, :, vcols]], axis=0)
-            query = q_ref[rows, cols]
-            cot = c_ref[rows, cols]
-            scores = dot(query, keys, 1, 1) * factor
-            top = jnp.max(scores, axis=-1, keepdims=True)
-            raised = jnp.exp(scores - top)
-            probs = raised / jnp.sum(raised, axis=-1, keepdims=True)
-            probs_b = probs.astype(jnp.bfloat16)
-            dprobs = dot(cot, values, 1, 1)
-            delta = jnp.sum(probs * dprobs, axis=-1, keepdims=True)
-            dscores = (probs * (dprobs - delta) * factor).astype(jnp.bfloat16)
-            key_grad = dot(dscores, query, 0, 0)
-            value_grad = dot(probs_b, cot, 0, 0)
-            grads[first, :, cols] += key_grad[:NROWS]
-            grads[second, :, cols] += key_grad[NROWS:]
-            grads[first, :, vcols] += value_grad[:NROWS]
-            grads[second, :, vcols] += value_grad[NROWS:]
-
-            @pl.when(owner == me)
-            def _():
-                own = pl.ds(pl.multiple_of(inner * SPAN, SPAN), SPAN)
-                att_ref[own, cols] = dot(probs_b, values, 1, 0).astype(jnp.bfloat16)
-                qg_ref[own, cols] = dot(dscores, keys, 1, 0).astype(jnp.bfloat16)
+            side = jnp.concatenate(
+                [
+                    jnp.concatenate([q_ref[rows, cols], zeros], axis=1),
+                    jnp.concatenate([zeros, c_ref[rows, cols]], axis=1),
+                ],
+                axis=0,
+            )
+            keyed = jnp.concatenate([proj[first, :, both[h]], proj[second, :, both[h]]], axis=0)
+            sides.append(side)
+            products.append(dot(side, keyed, 1, 1))
+        scores = jnp.concatenate([x[:SPAN] for x in products], axis=0) * factor
+        dprobs = jnp.concatenate([x[SPAN:] for x in products], axis=0)
+        top = jnp.max(scores, axis=-1, keepdims=True)
+        raised = jnp.exp(scores - top)
+        probs = raised * (1.0 / jnp.sum(raised, axis=-1, keepdims=True))
+        delta = jnp.sum(probs * dprobs, axis=-1, keepdims=True)
+        dscores = (probs * (dprobs - delta) * factor).astype(jnp.bfloat16)
+        probs_b = probs.astype(jnp.bfloat16)
+        totals = []
+        for h in range(heads):
+            part = slice(h * SPAN, (h + 1) * SPAN)
+            stacked = jnp.concatenate([dscores[part], probs_b[part]], axis=0)
+            kept[span, h] = stacked
+            totals.append(dot(stacked, sides[h], 0, 0))
+        for h in range(heads):
+            grads[first, :, both[h]] += totals[h][:NROWS]
+        for h in range(heads):
+            grads[second, :, both[h]] += totals[h][NROWS:]
+
+    for inner in range(spans_dev):
+        first = p_ref[me, 0, inner * NBR]
+        second = p_ref[me, 0, inner * NBR + 1]
+        own = slice(inner * SPAN, (inner + 1) * SPAN)
+        for h in range(heads):
+            cols = slice(h * HD, (h + 1) * HD)
+            both_h = slice(2 * h * HD, 2 * (h + 1) * HD)
+            keyed = jnp.concatenate([proj[first, :, both_h], proj[second, :, both_h]], axis=0)
+            product = dot(kept[me * spans_dev + inner, h], keyed, 1, 0)
+            qg_ref[own, cols] = product[:SPAN, :HD].astype(jnp.bfloat16)
+            att_ref[own, cols] = product[SPAN:, HD:].astype(jnp.bfloat16)
 
     @pl.loop(0, n)
     def _(block):
-        grads_b[pl.ds(block * rows_dev, rows_dev), :] = grads[block].astype(jnp.bfloat16)
+        rows = pl.ds(block * rows_dev, rows_dev)
+        for h in range(heads):
+            for t in range(2):
+                grads_b[rows, t * width + h * HD : t * width + (h + 1) * HD] = grads[
+                    block, :, (2 * h + t) * HD : (2 * h + t + 1) * HD
+                ].astype(jnp.bfloat16)
 
     own_grads = grads_b[pl.ds(me * rows_dev, rows_dev), :]
     partial = dot(own_grads, w_ref[...], 1, 1).astype(jnp.bfloat16)
@@ -225,20 +253,23 @@
         == lax.broadcasted_iota(jnp.int32, (depth, enc), 1)
     ).astype(jnp.bfloat16)
     columns = dot(picked, e_ref[...], 1, 1).astype(jnp.bfloat16)
-    wg_ref[...] = dot(columns, grads_b[...], 1, 0)
+    product = dot(columns, grads_b[...], 1, 0)
+    for t in range(2):
+        wg_ref[:, t, :] = product[:, t * width : (t + 1) * width]
 
 
 def local_part(n, m, p, w, e, q, c):
     vmem = pl.BlockSpec(memory_space=pltpu.VMEM)
     depth, width = w.shape[0] // n, q.shape[1]
     rows, tokens, enc = e.shape[0] // n, q.shape[0] // n, e.shape[1]
+    heads = width // HD
     return pl.pallas_call(
         functools.partial(local_kernel, n, m),
         out_shape=[
             jax.ShapeDtypeStruct((tokens, width), jnp.bfloat16),
             jax.ShapeDtypeStruct((tokens, width), jnp.bfloat16),
             jax.ShapeDtypeStruct((m, rows, enc // m), jnp.bfloat16),
-            jax.ShapeDtypeStruct((depth, 2 * width), jnp.float32),
+            jax.ShapeDtypeStruct((depth, 2, width), jnp.float32),
         ],
         in_specs=[pl.BlockSpec(memory_space=pltpu.SMEM)] + [vmem] * 4,
         out_specs=[vmem] * 4,
@@ -246,6 +277,7 @@
             pltpu.VMEM((n, rows, 2 * width), jnp.bfloat16),
             pltpu.VMEM((n, rows, 2 * width), jnp.float32),
             pltpu.VMEM((n * rows, 2 * width), jnp.bfloat16),
+            pltpu.VMEM((n * tokens // SPAN, heads, 2 * SPAN, NBR * NROWS), jnp.bfloat16),
         ],
         compiler_params=pltpu.CompilerParams(vmem_limit_bytes=VMEM_BYTES),
         name="attention_and_gradients",
@@ -314,7 +346,7 @@
         c.reshape(-1, width),
     )
     encoding_grad = group_sum(m, part)
-    return attended, query_grad, encoding_grad, weight_grad.reshape(depth, 2, width)
+    return attended, query_grad, encoding_grad, weight_grad
 
 
 def shifted(value, axis, steps):

time: 118 us -> 88 us (0.75)
  Pallas kernels: 110 us -> 82.2 us
  local copies, waits for them, and re-layouts: 6.74 us -> 4.58 us
    pallas_call x1, Pallas kernels: 50.9 us -> 23.4 us  [local_part(): pl.pallas_call(functools.partial(local_kernel, n, m), out_shape=[jax.Shap...]
    reshape x1 -> x0, local copies, waits for them, and re-layouts: 2.17 us -> none  [per_device_gathered(): weight_grad.reshape(depth, 2, width)]
where the time goes in v2:
time: 88 us; the launch traced here: 87.5 us
  Pallas kernels  82.2 us (93%)
  local copies, waits for them, and re-layouts  4.58 us (5%)
    pallas_call x1, Pallas kernels, gather(): pl.pallas_call(functools.partial(gather_kernel, n, m), out_shape=[jax.Sha...  52.2 us
    pallas_call x1, Pallas kernels, local_part(): pl.pallas_call(functools.partial(local_kernel, n, m), out_shape=[jax.Shap...  23.4 us
    pallas_call x1, Pallas kernels, group_sum(): pl.pallas_call(functools.partial(group_sum_kernel, m), out_shape=jax.Shap...  6.59 us
    unnamed x2, local copies, waits for them, and re-layouts  3.22 us

profile of v2, /device:TPU:0, one launch (start us, length us, event | category | flops | bytes accessed | tf_op | source)
XLA Modules:
  0.0 87.5 jit_solution(5491710413327351492)
XLA Ops:
  0.6 0.8 reshape.27
  1.4 0.6 pad.4.p_ref
  2.0 1.7 %copy.10 = bf16[14,8,2,512]{3,1,2,0:T(8,128)(2,1)} copy(bf16[14,8,2,512]{3,2,1,0:T(2,128)(2,1)} %bitcast.11) | data formatting | bytes 458752
  3.6 52.2 %gather_inputs.1 = (bf16[8,112,1024]{2,1,0:T(8,128)(2,1)}, bf16[8,128,896]{2,1,0:T(8,128)(2,1)}, bf16[8,128,512]{2,1,0:T(8,128)(2,1)}, bf16[8,128,512]{2,1,0:T(8,128)(2,1)}, s32[8,8,128]{2,1,0:T(8,128)}) custom-call(bf16[112,1024]{1,0:T(8,128)(2,1)} %bitcast.10, bf16[128,896]{1,0:T(8,128)(2,1)} %e_ref.1, bf16[128,512]{1,0:T(8,128)(2,1)} %q_ref.1, ...), custom_call_target="tpu_custom_call" | custom-call | tf_op jit(solution)/shard_map/gather_inputs/pallas_call | solution.py:140
  55.9 23.4 %attention_and_gradients.1 = (bf16[128,512]{1,0:T(8,128)(2,1)}, bf16[128,512]{1,0:T(8,128)(2,1)}, bf16[4,128,224]{2,1,0:T(8,128)(2,1)}, f32[112,2,512]{2,1,0:T(2,128)}) custom-call(s32[8,8,128]{2,1,0:T(8,128)} %get-tuple-element.13.p_ref, bf16[896,1024]{1,0:T(8,128)(2,1)} %bitcast.6, bf16[1024,896]{1,0:T(8,128)(2,1)} %bitcast.7, bf16[1024,512]{1,0:T(8,128)(2,1)} %bitcast.8, ...), custom_call_target="tpu_custom_call" | custom-call | tf_op jit(solution)/shard_map/attention_and_gradients/pallas_call | solution.py:266
  79.3 6.6 %group_sum.1 = bf16[128,224]{1,0:T(8,128)(2,1)} custom-call(bf16[4,128,224]{2,1,0:T(8,128)(2,1)} %get-tuple-element.20.part_ref), custom_call_target="tpu_custom_call" | custom-call | tf_op jit(solution)/shard_map/group_sum/pallas_call | solution.py:318
  85.9 1.6 %copy.9 = bf16[128,224]{0,1:T(8,128)(2,1)} copy(bf16[128,224]{1,0:T(8,128)(2,1)} %group_sum.1) | data formatting | bytes 114688

commit v3 on v0

--- a/solution.py
+++ b/solution.py
@@ -1,6 +1,10 @@
+import functools
+
 import jax
 import jax.numpy as jnp
 from jax import lax
+from jax.experimental import pallas as pl
+from jax.experimental.pallas import tpu as pltpu
 from jax.sharding import PartitionSpec as P
 
 HD = 128
@@ -8,7 +12,350 @@
 NROWS = 128
 NBR = 2
 REACH = 2
-
+GATHER_LIMIT = 8
+VMEM_BYTES = 56 * 1024 * 1024
+MESH = pl.DeviceIdType.MESH
+
+
+def whole_kernel(
+    n, m, w_ref, e_ref, q_ref, c_ref, p_ref, att_ref, qg_ref, eg_ref, wg_ref,
+    w_all, e_all, q_all, c_all, p_all, pids, order, previous, latest,
+    proj, chain, grads_b, parts, landed,
+    send_sems, recv_sems, share_send, share_recv, own_sems, sum_send, sum_recv,
+):
+    me = lax.axis_index("dp")
+    mp = lax.axis_index("mp")
+    half = n // 2
+    depth = me // 2
+    side = me % 2
+    ring = depth + side * (n - 1 - 2 * depth)
+    part = e_all.shape[1] // m
+
+    def at(position):
+        position = (position + 2 * n) % n
+        upper = position // half
+        return (1 - upper) * 2 * position + upper * (2 * (n - 1 - position) + 1)
+
+    targets = (at(ring + 1), at(ring - 1))
+    barrier = pltpu.get_barrier_semaphore()
+    for target in targets:
+        pl.semaphore_signal(barrier, inc=1, device_id=(target, mp), device_id_type=MESH)
+    for k in range(1, m):
+        pl.semaphore_signal(barrier, inc=1, device_id=(me, (mp + k) % m), device_id_type=MESH)
+    pl.semaphore_wait(barrier, m + 1)
+
+    own_rows = pl.ds(mp * part, part)
+    sources = (w_ref, e_ref.at[own_rows], p_ref, q_ref, c_ref)
+
+    def view(a, slot):
+        if a == 1:
+            return e_all.at[slot, own_rows]
+        return (w_all, None, p_all, q_all, c_all)[a].at[slot]
+
+    def travels(d, step, a):
+        if step < half:
+            return True
+        return step == half and (a < 3) == (d == 0)
+
+    def slot_of(d, step):
+        return at(ring - step) if d == 0 else at(ring + step)
+
+    def send(d, step, a):
+        slot = slot_of(d, step - 1)
+        return pltpu.make_async_remote_copy(
+            src_ref=sources[a] if step == 1 else view(a, slot),
+            dst_ref=view(a, slot),
+            send_sem=send_sems.at[d, step - 1, a],
+            recv_sem=recv_sems.at[d, step - 1, a],
+            device_id=(targets[d], mp),
+            device_id_type=MESH,
+        )
+
+    def arrival(d, step, a):
+        slot = slot_of(d, step)
+        return pltpu.make_async_remote_copy(
+            src_ref=view(a, slot),
+            dst_ref=view(a, slot),
+            send_sem=send_sems.at[d, step - 1, a],
+            recv_sem=recv_sems.at[d, step - 1, a],
+            device_id=(targets[d], mp),
+            device_id_type=MESH,
+        )
+
+    def share(d, step, k, arriving):
+        slot = slot_of(d, step)
+        row = (mp + m - k) % m if arriving else mp
+        block = e_all.at[slot, pl.ds(row * part, part)]
+        return pltpu.make_async_remote_copy(
+            src_ref=block,
+            dst_ref=block,
+            send_sem=share_send.at[d, step - 1, k - 1],
+            recv_sem=share_recv.at[d, step - 1, k - 1],
+            device_id=(me, (mp + k) % m),
+            device_id_type=MESH,
+        )
+
+    sent = []
+    shared = []
+
+    def start(d, step, a):
+        copy = send(d, step, a)
+        copy.start()
+        sent.append(copy)
+
+    def pass_on(step, arrays):
+        for a in arrays:
+            for d in range(2):
+                if not travels(d, step, a):
+                    continue
+                arrival(d, step, a).wait_recv()
+                if travels(d, step + 1, a):
+                    start(d, step + 1, a)
+                if a == 1:
+                    for k in range(1, m):
+                        copy = share(d, step, k, False)
+                        copy.start()
+                        shared.append((copy, d, step, k))
+
+    first_arrays, later_arrays = (2, 0, 1), (3, 4)
+    for a in first_arrays + later_arrays:
+        for d in range(2):
+            start(d, 1, a)
+    own = [
+        pltpu.make_async_copy(source, whole.at[me], own_sems.at[i])
+        for i, (source, whole) in enumerate(
+            ((w_ref, w_all), (e_ref, e_all), (p_ref, p_all), (q_ref, q_all), (c_ref, c_all))
+        )
+    ]
+    for copy in own:
+        copy.start()
+
+    heads = q_all.shape[2] // HD
+    width = heads * HD
+    spans_dev = q_all.shape[1] // SPAN
+    rows_dev = e_all.shape[1]
+    pair_count = n * spans_dev * NBR
+    factor = 1.0 / HD**0.5
+    zeros = jnp.zeros((SPAN, HD), jnp.bfloat16)
+    chain[pair_count] = jnp.zeros(chain.shape[1:], jnp.float32)
+    for copy in own:
+        copy.wait()
+
+    for step in range(1, half):
+        pass_on(step, first_arrays)
+        if step == half - 2:
+            pass_on(1, later_arrays)
+    pass_on(half, first_arrays)
+    for _, d, step, k in shared:
+        share(d, step, k, True).wait_recv()
+
+    to_scalars = pltpu.make_async_copy(p_all, pids, own_sems.at[5])
+    to_scalars.start()
+
+    @pl.loop(0, n)
+    def _(block):
+        rows = dot(
+            e_all[block], w_all[...].reshape(n * w_all.shape[1], 2 * width), 1, 0
+        ).astype(jnp.bfloat16)
+        for h in range(heads):
+            for t in range(2):
+                proj[block, :, (2 * h + t) * HD : (2 * h + t + 1) * HD] = rows[
+                    :, t * width + h * HD : t * width + (h + 1) * HD
+                ]
+
+    to_scalars.wait()
+
+    def owner_of(unit):
+        hops = (unit + 1) // 2
+        return at(ring + hops * (2 * ((unit + 1) % 2) - 1))
+
+    def link(index, last):
+        unit = index // (spans_dev * NBR)
+        block = pids[owner_of(unit), 0, index % (spans_dev * NBR)]
+        order[index] = block
+        before = jnp.int32(pair_count)
+        for number in range(n):
+            before = jnp.where(block == number, last[number], before)
+        previous[index] = before
+        return tuple(jnp.where(block == number, index, last[number]) for number in range(n))
+
+    last = lax.fori_loop(0, pair_count, link, (jnp.int32(pair_count),) * n)
+    for number in range(n):
+        latest[number] = last[number]
+
+    def attend(unit_base, units, is_own):
+        @pl.loop(0, units * spans_dev)
+        def _(index):
+            unit = unit_base + index // spans_dev
+            inner = index % spans_dev
+            owner = owner_of(unit)
+            pair = (unit * spans_dev + inner) * NBR
+            first, second = order[pair], order[pair + 1]
+            before_first, before_second = previous[pair], previous[pair + 1]
+            rows = pl.ds(pl.multiple_of(inner * SPAN, SPAN), SPAN)
+            both = [slice(2 * h * HD, 2 * (h + 1) * HD) for h in range(heads)]
+            sides, products = [], []
+            for h in range(heads):
+                cols = slice(h * HD, (h + 1) * HD)
+                side = jnp.concatenate(
+                    [
+                        jnp.concatenate([q_all[owner, rows, cols], zeros], axis=1),
+                        jnp.concatenate([zeros, c_all[owner, rows, cols]], axis=1),
+                    ],
+                    axis=0,
+                )
+                keyed = jnp.concatenate(
+                    [proj[first, :, both[h]], proj[second, :, both[h]]], axis=0
+                )
+                sides.append(side)
+                products.append(dot(side, keyed, 1, 1))
+            scores = jnp.concatenate([x[:SPAN] for x in products], axis=0) * factor
+            dprobs = jnp.concatenate([x[SPAN:] for x in products], axis=0)
+            top = jnp.max(scores, axis=-1, keepdims=True)
+            raised = jnp.exp(scores - top)
+            probs = raised * (1.0 / jnp.sum(raised, axis=-1, keepdims=True))
+            delta = jnp.sum(probs * dprobs, axis=-1, keepdims=True)
+            dscores = (probs * (dprobs - delta) * factor).astype(jnp.bfloat16)
+            probs_b = probs.astype(jnp.bfloat16)
+            totals = []
+            for h in range(heads):
+                cut = slice(h * SPAN, (h + 1) * SPAN)
+                stacked = jnp.concatenate([dscores[cut], probs_b[cut]], axis=0)
+                totals.append(dot(stacked, sides[h], 0, 0))
+                if is_own:
+                    keyed = jnp.concatenate(
+                        [proj[first, :, both[h]], proj[second, :, both[h]]], axis=0
+                    )
+                    product = dot(stacked, keyed, 1, 0)
+                    cols = slice(h * HD, (h + 1) * HD)
+                    qg_ref[rows, cols] = product[:SPAN, :HD].astype(jnp.bfloat16)
+                    att_ref[rows, cols] = product[SPAN:, HD:].astype(jnp.bfloat16)
+            for h in range(heads):
+                chain[pair, :, both[h]] = totals[h][:NROWS] + chain[before_first, :, both[h]]
+            for h in range(heads):
+                chain[pair + 1, :, both[h]] = totals[h][NROWS:] + chain[before_second, :, both[h]]
+
+    attend(0, 1, True)
+    for step in range(1, half):
+        if step + 1 < half:
+            pass_on(step + 1, later_arrays)
+        attend(2 * step - 1, 2, False)
+    pass_on(half, later_arrays)
+    attend(n - 1, 1, False)
+
+    def settle(block):
+        at_end = latest[block]
+        rows = pl.ds(block * rows_dev, rows_dev)
+        for h in range(heads):
+            for t in range(2):
+                grads_b[rows, t * width + h * HD : t * width + (h + 1) * HD] = chain[
+                    at_end, :, (2 * h + t) * HD : (2 * h + t + 1) * HD
+                ].astype(jnp.bfloat16)
+
+    settle(me)
+    own_grads = grads_b[pl.ds(me * rows_dev, rows_dev), :]
+    weights = w_all[...].reshape(n * w_all.shape[1], 2 * width)
+    partial = dot(weights, own_grads, 1, 1).astype(jnp.bfloat16)
+    piece = parts.shape[1]
+    for k in range(m):
+        parts[k] = partial[k * piece : (k + 1) * piece]
+    copies = []
+    for k in range(1, m):
+        target = (mp + k) % m
+        copy = pltpu.make_async_remote_copy(
+            src_ref=parts.at[target],
+            dst_ref=landed.at[k - 1],
+            send_sem=sum_send.at[k - 1],
+            recv_sem=sum_recv.at[k - 1],
+            device_id=(me, target),
+            device_id_type=MESH,
+        )
+        copy.start()
+        copies.append(copy)
+
+    @pl.loop(1, n)
+    def _(offset):
+        settle((me + offset) % n)
+
+    depth, enc = wg_ref.shape[0], e_all.shape[2]
+    picked = (
+        lax.broadcasted_iota(jnp.int32, (depth, enc), 0) + me * depth
+        == lax.broadcasted_iota(jnp.int32, (depth, enc), 1)
+    ).astype(jnp.bfloat16)
+    columns = dot(picked, e_all[...].reshape(n * rows_dev, enc), 1, 1).astype(jnp.bfloat16)
+    product = dot(columns, grads_b[...], 1, 0)
+    for t in range(2):
+        wg_ref[:, t, :] = product[:, t * width : (t + 1) * width]
+
+    total = parts[mp].astype(jnp.float32)
+    for k in range(1, m):
+        copies[k - 1].wait_recv()
+        total = total + landed[k - 1].astype(jnp.float32)
+    eg_ref[...] = total.astype(eg_ref.dtype)
+    for copy in copies:
+        copy.wait_send()
+    for copy, d, step, k in shared:
+        copy.wait_send()
+    for copy in sent:
+        copy.wait_send()
+
+
+def dot(a, b, da, db):
+    return lax.dot_general(a, b, (((da,), (db,)), ((), ())), preferred_element_type=jnp.float32)
+
+
+def whole(n, m, w, e, q, c, p):
+    half = n // 2
+    any_spec = pl.BlockSpec(memory_space=pl.ANY)
+    vmem = pl.BlockSpec(memory_space=pltpu.VMEM)
+    depth, double = w.shape
+    width = q.shape[1]
+    rows, enc = e.shape
+    pair_count = n * (q.shape[0] // SPAN) * NBR
+    arrays = (w, e, q, c, p)
+    return pl.pallas_call(
+        functools.partial(whole_kernel, n, m),
+        out_shape=[
+            jax.ShapeDtypeStruct(q.shape, jnp.bfloat16),
+            jax.ShapeDtypeStruct(q.shape, jnp.bfloat16),
+            jax.ShapeDtypeStruct((enc // m, rows), jnp.bfloat16),
+            jax.ShapeDtypeStruct((depth, 2, width), jnp.float32),
+        ],
+        in_specs=[any_spec] * 5,
+        out_specs=[vmem] * 4,
+        scratch_shapes=[pltpu.VMEM((n,) + x.shape, x.dtype) for x in arrays]
+        + [
+            pltpu.SMEM((n,) + p.shape, jnp.int32),
+            pltpu.SMEM((pair_count,), jnp.int32),
+            pltpu.SMEM((pair_count,), jnp.int32),
+            pltpu.SMEM((n,), jnp.int32),
+            pltpu.VMEM((n, rows, double), jnp.bfloat16),
+            pltpu.VMEM((pair_count + 1, NROWS, double), jnp.float32),
+            pltpu.VMEM((n * rows, double), jnp.bfloat16),
+            pltpu.VMEM((m, enc // m, rows), jnp.bfloat16),
+            pltpu.VMEM((m - 1, enc // m, rows), jnp.bfloat16),
+            pltpu.SemaphoreType.DMA((2, half, 5)),
+            pltpu.SemaphoreType.DMA((2, half, 5)),
+            pltpu.SemaphoreType.DMA((2, half, m - 1)),
+            pltpu.SemaphoreType.DMA((2, half, m - 1)),
+            pltpu.SemaphoreType.DMA((6,)),
+            pltpu.SemaphoreType.DMA((m - 1,)),
+            pltpu.SemaphoreType.DMA((m - 1,)),
+        ],
+        compiler_params=pltpu.CompilerParams(
+            collective_id=0, has_side_effects=True, vmem_limit_bytes=VMEM_BYTES
+        ),
+        name="whole_step",
+    )(w, e, q, c, p)
+
+
+def per_device_gathered(n, m, queries, encodings, kv_weight, pair_list, cotangent):
+    depth, _, width = kv_weight.shape
+    pairs = jnp.pad(pair_list.reshape(1, -1), ((0, 7), (0, 128 - pair_list.size)))
+    attended, query_grad, encoding_grad, weight_grad = whole(
+        n, m, kv_weight.reshape(depth, 2 * width), encodings, queries, cotangent, pairs
+    )
+    return attended, query_grad, encoding_grad.T, weight_grad
 
 def shifted(value, axis, steps):
     count = lax.axis_size(axis)
@@ -119,8 +466,12 @@
 
 
 def solution(mesh):
+    n, m = mesh.shape["dp"], mesh.shape["mp"]
+    body = per_device
+    if n == GATHER_LIMIT:
+        body = functools.partial(per_device_gathered, n, m)
     return jax.shard_map(
-        per_device,
+        body,
         mesh=mesh,
         in_specs=(P("dp", "mp"), P("dp", None), P("dp", None, "mp"), P("dp", None), P("dp", "mp")),
         out_specs=(P("dp", "mp"), P("dp", "mp"), P("dp", "mp"), P("dp", None, "mp")),

time: 336 us -> 85.7 us (0.26)
  waiting for transfers between devices: 239 us -> 0 us
  Pallas kernels: 0 us -> 77.3 us
  local copies, waits for them, and re-layouts: 40.4 us -> 7.6 us
  matrix products: 23.1 us -> 0 us
  between operations: 14.6 us -> 0.66 us
  starting transfers between devices: 13.8 us -> 0 us
  other arithmetic: 4.91 us -> 0 us
    unnamed x4 -> x0, waiting for transfers between devices: 131 us -> none
    pallas_call x0 -> x1, Pallas kernels: none -> 77.3 us  [whole(): pl.pallas_call(functools.partial(whole_kernel, n, m), out_shape=[jax.Shap...]
    all_gather x1 -> x0, waiting for transfers between devices: 49.8 us -> none  [per_device(): weights = lax.all_gather(kv_weight, 'dp', axis=0, tiled=True)]
    ppermute x8 -> x0, waiting for transfers between devices: 37.8 us -> none  [shifted(): return lax.ppermute(value, axis, pairs)]
    dot_general x10 -> x0, matrix products: 23.1 us -> none  [the longest x1 5.67 us: per_device(): jnp.einsum('chqk,cqhd->ckhd', dscores, query_rows, preferred_element_type...]
    reduce_scatter x1 -> x0, waiting for transfers between devices: 20.1 us -> none  [per_device(): lax.psum_scatter(partial_sum.astype(jnp.bfloat16), 'mp', scatter_dimensio...]
    ppermute x8 -> x0, starting transfers between devices: 13.7 us -> none  [shifted(): return lax.ppermute(value, axis, pairs)]
    reshape x5 -> x1, local copies, waits for them, and re-layouts: 11 us -> 0.08 us  [per_device_gathered(): pair_list.reshape(1, -1)]
  transfers between devices with their start and end apart: 11 -> 0, of which waited for: 10 -> 0; matrix products, arithmetic and copies ran while one was open for 5% -> 0% of each run, Pallas kernels for 0% -> 0%
where the time goes in v3:
time: 85.7 us; the launch traced here: 85.5 us
  Pallas kernels  77.3 us (90%)
  local copies, waits for them, and re-layouts  7.6 us (9%)
    pallas_call x1, Pallas kernels, whole(): pl.pallas_call(functools.partial(whole_kernel, n, m), out_shape=[jax.Shap...  77.3 us
    unnamed x11, local copies, waits for them, and re-layouts  6.92 us

profile of v3, /device:TPU:0, one launch (start us, length us, event | category | flops | bytes accessed | tf_op | source)
XLA Modules:
  0.0 85.5 jit_solution(8760922860515042338)
XLA Ops:
  0.6 0.0 copy-start.2
  0.6 0.7 copy-done.2
  1.3 0.1 reshape.15
  1.4 0.6 pad.4.p_ref
  2.0 1.7 %copy.9 = bf16[14,8,2,512]{3,1,2,0:T(8,128)(2,1)} copy(bf16[14,8,2,512]{3,2,1,0:T(2,128)(2,1)} %bitcast.4) | data formatting | bytes 458752
  3.6 77.3 %whole_step.1 = (bf16[128,512]{1,0:T(8,128)(2,1)}, bf16[128,512]{1,0:T(8,128)(2,1)}, bf16[224,128]{1,0:T(8,128)(2,1)}, f32[112,2,512]{2,1,0:T(2,128)}) custom-call(bf16[112,1024]{1,0:T(8,128)(2,1)} %bitcast.3, bf16[128,896]{1,0:T(8,128)(2,1)} %e_ref.1, bf16[128,512]{1,0:T(8,128)(2,1)} %q_ref.1, bf16[128,512]{1,0:T(8,128)(2,1)} %c_ref.1, s32[8,128]{1,0:T(8,128)} %pad.4.p_ref), custom_call_target="tpu_custom_call" | custom-call | tf_op jit(solution)/shard_map/whole_step/pallas_call | solution.py:316
  80.9 0.0 copy-start
  80.9 1.6 %copy.14 = bf16[128,512]{1,0:T(8,128)(2,1)} copy(bf16[128,512]{1,0:T(8,128)(2,1)} %get-tuple-element.16) | data formatting | bytes 262144
  82.5 0.0 copy-start.1
  82.6 1.6 %copy.15 = bf16[128,512]{1,0:T(8,128)(2,1)} copy(bf16[128,512]{1,0:T(8,128)(2,1)} %get-tuple-element.17) | data formatting | bytes 262144
  84.1 0.0 copy-done.1
  84.1 0.6 copy.16
  84.8 0.0 copy-done
  84.8 0.8 copy.17
Async XLA Ops:
  0.6 0.7 copy-start.2
  80.9 3.8 %copy-start = (f32[112,2,512]{2,1,0:T(2,128)S(1)}, f32[112,2,512]{2,1,0:T(2,128)}, u32[]{:S(2)}) copy-start(f32[112,2,512]{2,1,0:T(2,128)} %get-tuple-element.19) | copy-start | bytes 1376260
  82.5 1.6 %copy-start.1 = (bf16[224,128]{1,0:T(8,128)(2,1)S(1)}, bf16[224,128]{1,0:T(8,128)(2,1)}, u32[]{:S(2)}) copy-start(bf16[224,128]{1,0:T(8,128)(2,1)} %get-tuple-element.10) | copy-start | bytes 172036

commit v4 on v3

--- a/solution.py
+++ b/solution.py
@@ -42,20 +42,40 @@
         pl.semaphore_signal(barrier, inc=1, device_id=(target, mp), device_id_type=MESH)
     for k in range(1, m):
         pl.semaphore_signal(barrier, inc=1, device_id=(me, (mp + k) % m), device_id_type=MESH)
+    own = [
+        pltpu.make_async_copy(source, whole.at[me], own_sems.at[i])
+        for i, (source, whole) in enumerate(((e_ref, e_all), (q_ref, q_all), (c_ref, c_all)))
+    ]
+    for copy in own:
+        copy.start()
+    tile = lax.broadcasted_iota(jnp.int32, p_all.shape[1:], 1)
+    listed = jnp.zeros(p_all.shape[1:], jnp.int32)
+    for k in range(p_ref.shape[0] * NBR):
+        listed = jnp.where(tile == k, p_ref[k // NBR, k % NBR], listed)
+    p_all[me] = listed
+    for t in range(2):
+        span_cols = w_ref.shape[2]
+        w_all[me, :, t * span_cols : (t + 1) * span_cols] = w_ref[:, t, :]
     pl.semaphore_wait(barrier, m + 1)
 
     own_rows = pl.ds(mp * part, part)
-    sources = (w_ref, e_ref.at[own_rows], p_ref, q_ref, c_ref)
+    first_arrays, later_arrays = (2, 0, 5, 1), (3, 4)
+    cut = w_all.shape[1] // 32 * 16
+    sources = (None, e_ref.at[own_rows], None, q_ref, c_ref, None)
 
     def view(a, slot):
+        if a == 0:
+            return w_all.at[slot, pl.ds(0, cut)]
+        if a == 5:
+            return w_all.at[slot, pl.ds(cut, w_all.shape[1] - cut)]
         if a == 1:
             return e_all.at[slot, own_rows]
-        return (w_all, None, p_all, q_all, c_all)[a].at[slot]
+        return (p_all, q_all, c_all)[a - 2].at[slot]
 
     def travels(d, step, a):
         if step < half:
             return True
-        return step == half and (a < 3) == (d == 0)
+        return step == half and (a not in later_arrays) == (d == 0)
 
     def slot_of(d, step):
         return at(ring - step) if d == 0 else at(ring + step)
@@ -63,7 +83,7 @@
     def send(d, step, a):
         slot = slot_of(d, step - 1)
         return pltpu.make_async_remote_copy(
-            src_ref=sources[a] if step == 1 else view(a, slot),
+            src_ref=view(a, slot) if step > 1 or sources[a] is None else sources[a],
             dst_ref=view(a, slot),
             send_sem=send_sems.at[d, step - 1, a],
             recv_sem=recv_sems.at[d, step - 1, a],
@@ -103,9 +123,9 @@
         copy.start()
         sent.append(copy)
 
-    def pass_on(step, arrays):
+    def pass_on(step, arrays, directions=(0, 1)):
         for a in arrays:
-            for d in range(2):
+            for d in directions:
                 if not travels(d, step, a):
                     continue
                 arrival(d, step, a).wait_recv()
@@ -117,18 +137,9 @@
                         copy.start()
                         shared.append((copy, d, step, k))
 
-    first_arrays, later_arrays = (2, 0, 1), (3, 4)
-    for a in first_arrays + later_arrays:
+    for a in first_arrays:
         for d in range(2):
             start(d, 1, a)
-    own = [
-        pltpu.make_async_copy(source, whole.at[me], own_sems.at[i])
-        for i, (source, whole) in enumerate(
-            ((w_ref, w_all), (e_ref, e_all), (p_ref, p_all), (q_ref, q_all), (c_ref, c_all))
-        )
-    ]
-    for copy in own:
-        copy.start()
 
     heads = q_all.shape[2] // HD
     width = heads * HD
@@ -143,31 +154,37 @@
 
     for step in range(1, half):
         pass_on(step, first_arrays)
-        if step == half - 2:
-            pass_on(1, later_arrays)
+    for a in later_arrays:
+        for d in (1, 0):
+            start(d, 1, a)
     pass_on(half, first_arrays)
     for _, d, step, k in shared:
         share(d, step, k, True).wait_recv()
 
-    to_scalars = pltpu.make_async_copy(p_all, pids, own_sems.at[5])
+    to_scalars = pltpu.make_async_copy(p_all, pids, own_sems.at[3])
     to_scalars.start()
 
-    @pl.loop(0, n)
-    def _(block):
-        rows = dot(
-            e_all[block], w_all[...].reshape(n * w_all.shape[1], 2 * width), 1, 0
-        ).astype(jnp.bfloat16)
-        for h in range(heads):
-            for t in range(2):
-                proj[block, :, (2 * h + t) * HD : (2 * h + t + 1) * HD] = rows[
-                    :, t * width + h * HD : t * width + (h + 1) * HD
-                ]
+    def project(start_block, end_block):
+        @pl.loop(start_block, end_block)
+        def _(block):
+            rows = dot(
+                e_all[block], w_all[...].reshape(n * w_all.shape[1], 2 * width), 1, 0
+            ).astype(jnp.bfloat16)
+            for h in range(heads):
+                for t in range(2):
+                    proj[block, :, (2 * h + t) * HD : (2 * h + t + 1) * HD] = rows[
+                        :, t * width + h * HD : t * width + (h + 1) * HD
+                    ]
+
+    project(0, half)
+    pass_on(1, later_arrays, (1,))
+    project(half, n)
 
     to_scalars.wait()
 
     def owner_of(unit):
         hops = (unit + 1) // 2
-        return at(ring + hops * (2 * ((unit + 1) % 2) - 1))
+        return at(ring + hops * (1 - 2 * ((unit + 1) % 2)))
 
     def link(index, last):
         unit = index // (spans_dev * NBR)
@@ -237,10 +254,10 @@
 
     attend(0, 1, True)
     for step in range(1, half):
-        if step + 1 < half:
-            pass_on(step + 1, later_arrays)
-        attend(2 * step - 1, 2, False)
-    pass_on(half, later_arrays)
+        pass_on(step, later_arrays, (0,))
+        attend(2 * step - 1, 1, False)
+        pass_on(step + 1, later_arrays, (1,))
+        attend(2 * step, 1, False)
     attend(n - 1, 1, False)
 
     def settle(block):
@@ -308,11 +325,12 @@
     half = n // 2
     any_spec = pl.BlockSpec(memory_space=pl.ANY)
     vmem = pl.BlockSpec(memory_space=pltpu.VMEM)
-    depth, double = w.shape
-    width = q.shape[1]
+    depth, _, width = w.shape
+    double = 2 * width
     rows, enc = e.shape
     pair_count = n * (q.shape[0] // SPAN) * NBR
-    arrays = (w, e, q, c, p)
+    listed = jax.ShapeDtypeStruct((8, 128), jnp.int32)
+    arrays = (jax.ShapeDtypeStruct((depth, double), w.dtype), e, q, c, listed)
     return pl.pallas_call(
         functools.partial(whole_kernel, n, m),
         out_shape=[
@@ -321,11 +339,11 @@
             jax.ShapeDtypeStruct((enc // m, rows), jnp.bfloat16),
             jax.ShapeDtypeStruct((depth, 2, width), jnp.float32),
         ],
-        in_specs=[any_spec] * 5,
+        in_specs=[vmem] + [any_spec] * 3 + [pl.BlockSpec(memory_space=pltpu.SMEM)],
         out_specs=[vmem] * 4,
         scratch_shapes=[pltpu.VMEM((n,) + x.shape, x.dtype) for x in arrays]
         + [
-            pltpu.SMEM((n,) + p.shape, jnp.int32),
+            pltpu.SMEM((n,) + listed.shape, jnp.int32),
             pltpu.SMEM((pair_count,), jnp.int32),
             pltpu.SMEM((pair_count,), jnp.int32),
             pltpu.SMEM((n,), jnp.int32),
@@ -334,11 +352,11 @@
             pltpu.VMEM((n * rows, double), jnp.bfloat16),
             pltpu.VMEM((m, enc // m, rows), jnp.bfloat16),
             pltpu.VMEM((m - 1, enc // m, rows), jnp.bfloat16),
-            pltpu.SemaphoreType.DMA((2, half, 5)),
-            pltpu.SemaphoreType.DMA((2, half, 5)),
+            pltpu.SemaphoreType.DMA((2, half, 6)),
+            pltpu.SemaphoreType.DMA((2, half, 6)),
             pltpu.SemaphoreType.DMA((2, half, m - 1)),
             pltpu.SemaphoreType.DMA((2, half, m - 1)),
-            pltpu.SemaphoreType.DMA((6,)),
+            pltpu.SemaphoreType.DMA((4,)),
             pltpu.SemaphoreType.DMA((m - 1,)),
             pltpu.SemaphoreType.DMA((m - 1,)),
         ],
@@ -350,10 +368,8 @@
 
 
 def per_device_gathered(n, m, queries, encodings, kv_weight, pair_list, cotangent):
-    depth, _, width = kv_weight.shape
-    pairs = jnp.pad(pair_list.reshape(1, -1), ((0, 7), (0, 128 - pair_list.size)))
     attended, query_grad, encoding_grad, weight_grad = whole(
-        n, m, kv_weight.reshape(depth, 2 * width), encodings, queries, cotangent, pairs
+        n, m, kv_weight, encodings, queries, cotangent, pair_list
     )
     return attended, query_grad, encoding_grad.T, weight_grad
 

time: 85.7 us -> 75.8 us (0.88)
  Pallas kernels: 77.3 us -> 70.3 us
  local copies, waits for them, and re-layouts: 7.6 us -> 4.59 us
    pallas_call x1, Pallas kernels: 77.3 us -> 70.3 us  [whole(): pl.pallas_call(functools.partial(whole_kernel, n, m), out_shape=[jax.Shap...]
    unnamed x11 -> x8, local copies, waits for them, and re-layouts: 6.92 us -> 4.59 us
where the time goes in v4:
time: 75.8 us; the launch traced here: 75.6 us
  Pallas kernels  70.3 us (93%)
  local copies, waits for them, and re-layouts  4.59 us (6%)
    pallas_call x1, Pallas kernels, whole(): pl.pallas_call(functools.partial(whole_kernel, n, m), out_shape=[jax.Shap...  70.3 us
    unnamed x8, local copies, waits for them, and re-layouts  4.59 us

profile of v4, /device:TPU:0, one launch (start us, length us, event | category | flops | bytes accessed | tf_op | source)
XLA Modules:
  0.0 75.6 jit_solution(5961233020084618043)
XLA Ops:
  0.6 70.3 %whole_step.1 = (bf16[128,512]{1,0:T(8,128)(2,1)}, bf16[128,512]{1,0:T(8,128)(2,1)}, bf16[224,128]{1,0:T(8,128)(2,1)}, f32[112,2,512]{2,1,0:T(2,128)}) custom-call(bf16[112,2,512]{2,1,0:T(2,128)(2,1)} %w_ref.1, bf16[128,896]{1,0:T(8,128)(2,1)} %e_ref.1, bf16[128,512]{1,0:T(8,128)(2,1)} %q_ref.1, bf16[128,512]{1,0:T(8,128)(2,1)} %c_ref.1, s32[2,2]{1,0:T(2,128)} %p_ref.1), custom_call_target="tpu_custom_call" | custom-call | tf_op jit(solution)/shard_map/whole_step/pallas_call | solution.py:334
  71.0 0.0 copy-start
  71.0 1.6 %copy.13 = bf16[128,512]{1,0:T(8,128)(2,1)} copy(bf16[128,512]{1,0:T(8,128)(2,1)} %get-tuple-element.16) | data formatting | bytes 262144
  72.6 0.0 copy-start.1
  72.6 1.6 %copy.14 = bf16[128,512]{1,0:T(8,128)(2,1)} copy(bf16[128,512]{1,0:T(8,128)(2,1)} %get-tuple-element.17) | data formatting | bytes 262144
  74.2 0.0 copy-done.1
  74.2 0.6 copy.15
  74.8 0.0 copy-done
  74.8 0.8 %copy.16 = f32[112,2,512]{2,1,0:T(2,128)} copy(f32[112,2,512]{2,1,0:T(2,128)S(1)} %copy-done) | data formatting | bytes 917504
Async XLA Ops:
  71.0 3.8 %copy-start = (f32[112,2,512]{2,1,0:T(2,128)S(1)}, f32[112,2,512]{2,1,0:T(2,128)}, u32[]{:S(2)}) copy-start(f32[112,2,512]{2,1,0:T(2,128)} %get-tuple-element.19) | copy-start | bytes 1376260
  72.6 1.6 %copy-start.1 = (bf16[224,128]{1,0:T(8,128)(2,1)S(1)}, bf16[224,128]{1,0:T(8,128)(2,1)}, u32[]{:S(2)}) copy-start(bf16[224,128]{1,0:T(8,128)(2,1)} %get-tuple-element.10) | copy-start | bytes 172036

commit v5 on v4

--- a/solution.py
+++ b/solution.py
@@ -20,7 +20,7 @@
 def whole_kernel(
     n, m, w_ref, e_ref, q_ref, c_ref, p_ref, att_ref, qg_ref, eg_ref, wg_ref,
     w_all, e_all, q_all, c_all, p_all, pids, order, previous, latest,
-    proj, chain, grads_b, parts, landed,
+    proj, chain, grads_b, columns, parts, landed,
     send_sems, recv_sems, share_send, share_recv, own_sems, sum_send, sum_recv,
 ):
     me = lax.axis_index("dp")
@@ -75,7 +75,7 @@
     def travels(d, step, a):
         if step < half:
             return True
-        return step == half and (a not in later_arrays) == (d == 0)
+        return step == half and (a in (2, 3, 5)) == (d == 0)
 
     def slot_of(d, step):
         return at(ring - step) if d == 0 else at(ring + step)
@@ -176,9 +176,7 @@
                         :, t * width + h * HD : t * width + (h + 1) * HD
                     ]
 
-    project(0, half)
-    pass_on(1, later_arrays, (1,))
-    project(half, n)
+    project(0, n)
 
     to_scalars.wait()
 
@@ -254,10 +252,17 @@
 
     attend(0, 1, True)
     for step in range(1, half):
-        pass_on(step, later_arrays, (0,))
-        attend(2 * step - 1, 1, False)
-        pass_on(step + 1, later_arrays, (1,))
-        attend(2 * step, 1, False)
+        pass_on(step, later_arrays)
+        attend(2 * step - 1, 2, False)
+    depth, enc = wg_ref.shape[0], e_all.shape[2]
+    picked = (
+        lax.broadcasted_iota(jnp.int32, (depth, enc), 0) + me * depth
+        == lax.broadcasted_iota(jnp.int32, (depth, enc), 1)
+    ).astype(jnp.bfloat16)
+    columns[...] = dot(
+        picked, e_all[...].reshape(n * rows_dev, enc), 1, 1
+    ).astype(jnp.bfloat16)
+    pass_on(half, later_arrays)
     attend(n - 1, 1, False)
 
     def settle(block):
@@ -294,13 +299,7 @@
     def _(offset):
         settle((me + offset) % n)
 
-    depth, enc = wg_ref.shape[0], e_all.shape[2]
-    picked = (
-        lax.broadcasted_iota(jnp.int32, (depth, enc), 0) + me * depth
-        == lax.broadcasted_iota(jnp.int32, (depth, enc), 1)
-    ).astype(jnp.bfloat16)
-    columns = dot(picked, e_all[...].reshape(n * rows_dev, enc), 1, 1).astype(jnp.bfloat16)
-    product = dot(columns, grads_b[...], 1, 0)
+    product = dot(columns[...], grads_b[...], 1, 0)
     for t in range(2):
         wg_ref[:, t, :] = product[:, t * width : (t + 1) * width]
 
@@ -350,6 +349,7 @@
             pltpu.VMEM((n, rows, double), jnp.bfloat16),
             pltpu.VMEM((pair_count + 1, NROWS, double), jnp.float32),
             pltpu.VMEM((n * rows, double), jnp.bfloat16),
+            pltpu.VMEM((depth, n * rows), jnp.bfloat16),
             pltpu.VMEM((m, enc // m, rows), jnp.bfloat16),
             pltpu.VMEM((m - 1, enc // m, rows), jnp.bfloat16),
             pltpu.SemaphoreType.DMA((2, half, 6)),
@@ -367,9 +367,37 @@
     )(w, e, q, c, p)
 
 
+def hand_out_kernel(*refs):
+    count = len(refs) // 2
+    sems = refs[-1]
+    copies = [
+        pltpu.make_async_copy(refs[i], refs[count + i], sems.at[i]) for i in range(count)
+    ]
+    for copy in copies:
+        copy.start()
+    for copy in copies:
+        copy.wait()
+
+
+def hand_out(*arrays):
+    any_spec = pl.BlockSpec(memory_space=pl.ANY)
+    return pl.pallas_call(
+        hand_out_kernel,
+        out_shape=[jax.ShapeDtypeStruct(x.shape, x.dtype) for x in arrays],
+        in_specs=[any_spec] * len(arrays),
+        out_specs=[any_spec] * len(arrays),
+        scratch_shapes=[pltpu.SemaphoreType.DMA((len(arrays),))],
+        compiler_params=pltpu.CompilerParams(vmem_limit_bytes=62 * 1024 * 1024),
+        name="hand_out",
+    )(*arrays)
+
+
 def per_device_gathered(n, m, queries, encodings, kv_weight, pair_list, cotangent):
     attended, query_grad, encoding_grad, weight_grad = whole(
         n, m, kv_weight, encodings, queries, cotangent, pair_list
+    )
+    attended, query_grad, encoding_grad, weight_grad = hand_out(
+        attended, query_grad, encoding_grad, weight_grad
     )
     return attended, query_grad, encoding_grad.T, weight_grad
 

time: 75.8 us -> 94 us (1.24)
  Pallas kernels: 70.3 us -> 93.2 us
  local copies, waits for them, and re-layouts: 4.59 us -> 0 us
    pallas_call x0 -> x1, Pallas kernels: none -> 24.7 us  [hand_out(): pl.pallas_call(hand_out_kernel, out_shape=[jax.ShapeDtypeStruct(x.shape,...]
    unnamed x8 -> x0, local copies, waits for them, and re-layouts: 4.59 us -> none
    pallas_call x1, Pallas kernels: 70.3 us -> 68.5 us  [whole(): pl.pallas_call(functools.partial(whole_kernel, n, m), out_shape=[jax.Shap...]
where the time goes in v5:
time: 94 us; the launch traced here: 93.8 us
  Pallas kernels  93.2 us (99%)
    pallas_call x1, Pallas kernels, whole(): pl.pallas_call(functools.partial(whole_kernel, n, m), out_shape=[jax.Shap...  68.5 us
    pallas_call x1, Pallas kernels, hand_out(): pl.pallas_call(hand_out_kernel, out_shape=[jax.ShapeDtypeStruct(x.shape,...  24.7 us

profile of v5, /device:TPU:0, one launch (start us, length us, event | category | flops | bytes accessed | tf_op | source)
XLA Modules:
  0.0 93.8 jit_solution(12855140515863452324)
XLA Ops:
  0.6 68.5 %whole_step.1 = (bf16[128,512]{1,0:T(8,128)(2,1)}, bf16[128,512]{1,0:T(8,128)(2,1)}, bf16[224,128]{1,0:T(8,128)(2,1)}, f32[112,2,512]{2,1,0:T(2,128)}) custom-call(bf16[112,2,512]{2,1,0:T(2,128)(2,1)} %w_ref.1, bf16[128,896]{1,0:T(8,128)(2,1)} %e_ref.1, bf16[128,512]{1,0:T(8,128)(2,1)} %q_ref.1, bf16[128,512]{1,0:T(8,128)(2,1)} %c_ref.1, s32[2,2]{1,0:T(2,128)} %p_ref.1), custom_call_target="tpu_custom_call" | custom-call | tf_op jit(solution)/shard_map/whole_step/pallas_call | solution.py:333
  69.1 24.7 %hand_out.1 = (bf16[128,512]{1,0:T(8,128)(2,1)}, bf16[128,512]{1,0:T(8,128)(2,1)}, bf16[224,128]{1,0:T(8,128)(2,1)}, f32[112,2,512]{2,1,0:T(2,128)}) custom-call(bf16[128,512]{1,0:T(8,128)(2,1)} %get-tuple-element.12.refs_0_, bf16[128,512]{1,0:T(8,128)(2,1)} %get-tuple-element.13.refs_1_, bf16[224,128]{1,0:T(8,128)(2,1)} %get-tuple-element.14.refs_2_, ...), custom_call_target="tpu_custom_call" | custom-call | tf_op jit(solution)/shard_map/hand_out/pallas_call | solution.py:384

commit v6 on v5

--- a/solution.py
+++ b/solution.py
@@ -56,12 +56,13 @@
     for t in range(2):
         span_cols = w_ref.shape[2]
         w_all[me, :, t * span_cols : (t + 1) * span_cols] = w_ref[:, t, :]
+    for copy in own:
+        copy.wait()
     pl.semaphore_wait(barrier, m + 1)
 
     own_rows = pl.ds(mp * part, part)
     first_arrays, later_arrays = (2, 0, 5, 1), (3, 4)
     cut = w_all.shape[1] // 32 * 16
-    sources = (None, e_ref.at[own_rows], None, q_ref, c_ref, None)
 
     def view(a, slot):
         if a == 0:
@@ -83,7 +84,7 @@
     def send(d, step, a):
         slot = slot_of(d, step - 1)
         return pltpu.make_async_remote_copy(
-            src_ref=view(a, slot) if step > 1 or sources[a] is None else sources[a],
+            src_ref=view(a, slot),
             dst_ref=view(a, slot),
             send_sem=send_sems.at[d, step - 1, a],
             recv_sem=recv_sems.at[d, step - 1, a],
@@ -149,8 +150,6 @@
     factor = 1.0 / HD**0.5
     zeros = jnp.zeros((SPAN, HD), jnp.bfloat16)
     chain[pair_count] = jnp.zeros(chain.shape[1:], jnp.float32)
-    for copy in own:
-        copy.wait()
 
     for step in range(1, half):
         pass_on(step, first_arrays)
@@ -369,25 +368,18 @@
 
 def hand_out_kernel(*refs):
     count = len(refs) // 2
-    sems = refs[-1]
-    copies = [
-        pltpu.make_async_copy(refs[i], refs[count + i], sems.at[i]) for i in range(count)
-    ]
-    for copy in copies:
-        copy.start()
-    for copy in copies:
-        copy.wait()
+    for i in range(count):
+        refs[count + i][...] = refs[i][...]
 
 
 def hand_out(*arrays):
-    any_spec = pl.BlockSpec(memory_space=pl.ANY)
+    vmem = pl.BlockSpec(memory_space=pltpu.VMEM)
     return pl.pallas_call(
         hand_out_kernel,
         out_shape=[jax.ShapeDtypeStruct(x.shape, x.dtype) for x in arrays],
-        in_specs=[any_spec] * len(arrays),
-        out_specs=[any_spec] * len(arrays),
-        scratch_shapes=[pltpu.SemaphoreType.DMA((len(arrays),))],
-        compiler_params=pltpu.CompilerParams(vmem_limit_bytes=62 * 1024 * 1024),
+        in_specs=[vmem] * len(arrays),
+        out_specs=[vmem] * len(arrays),
+        compiler_params=pltpu.CompilerParams(vmem_limit_bytes=VMEM_BYTES),
         name="hand_out",
     )(*arrays)
 

time: 94 us -> 71.4 us (0.76)
  Pallas kernels: 93.2 us -> 70.6 us
    pallas_call x1, Pallas kernels: 24.7 us -> 2.07 us  [hand_out(): pl.pallas_call(hand_out_kernel, out_shape=[jax.ShapeDtypeStruct(x.shape,...]
where the time goes in v6:
time: 71.4 us; the launch traced here: 71.2 us
  Pallas kernels  70.6 us (99%)
    pallas_call x1, Pallas kernels, whole(): pl.pallas_call(functools.partial(whole_kernel, n, m), out_shape=[jax.Shap...  68.5 us
    pallas_call x1, Pallas kernels, hand_out(): pl.pallas_call(hand_out_kernel, out_shape=[jax.ShapeDtypeStruct(x.shape,...  2.07 us

profile of v6, /device:TPU:0, one launch (start us, length us, event | category | flops | bytes accessed | tf_op | source)
XLA Modules:
  0.0 71.2 jit_solution(13374885580643608685)
XLA Ops:
  0.6 68.5 %whole_step.1 = (bf16[128,512]{1,0:T(8,128)(2,1)}, bf16[128,512]{1,0:T(8,128)(2,1)}, bf16[224,128]{1,0:T(8,128)(2,1)}, f32[112,2,512]{2,1,0:T(2,128)}) custom-call(bf16[112,2,512]{2,1,0:T(2,128)(2,1)} %w_ref.1, bf16[128,896]{1,0:T(8,128)(2,1)} %e_ref.1, bf16[128,512]{1,0:T(8,128)(2,1)} %q_ref.1, bf16[128,512]{1,0:T(8,128)(2,1)} %c_ref.1, s32[2,2]{1,0:T(2,128)} %p_ref.1), custom_call_target="tpu_custom_call" | custom-call | tf_op jit(solution)/shard_map/whole_step/pallas_call | solution.py:332
  69.1 2.1 %hand_out.1 = (bf16[128,512]{1,0:T(8,128)(2,1)}, bf16[128,512]{1,0:T(8,128)(2,1)}, bf16[224,128]{1,0:T(8,128)(2,1)}, f32[112,2,512]{2,1,0:T(2,128)}) custom-call(bf16[128,512]{1,0:T(8,128)(2,1)} %get-tuple-element.12.refs_0_, bf16[128,512]{1,0:T(8,128)(2,1)} %get-tuple-element.13.refs_1_, bf16[224,128]{1,0:T(8,128)(2,1)} %get-tuple-element.14.refs_2_, ...), custom_call_target="tpu_custom_call" | custom-call | tf_op jit(solution)/shard_map/hand_out/pallas_call | solution.py:377

commit v7 on v6

--- a/solution.py
+++ b/solution.py
@@ -61,7 +61,7 @@
     pl.semaphore_wait(barrier, m + 1)
 
     own_rows = pl.ds(mp * part, part)
-    first_arrays, later_arrays = (2, 0, 5, 1), (3, 4)
+    first_arrays, later_arrays = (2, 1, 0, 5), (3, 4)
     cut = w_all.shape[1] // 32 * 16
 
     def view(a, slot):

time: 71.4 us -> 67.9 us (0.951)
  Pallas kernels: 70.6 us -> 67.1 us
    pallas_call x1, Pallas kernels: 68.5 us -> 65 us  [whole(): pl.pallas_call(functools.partial(whole_kernel, n, m), out_shape=[jax.Shap...]
where the time goes in v7:
time: 67.9 us; the launch traced here: 67.7 us
  Pallas kernels  67.1 us (99%)
    pallas_call x1, Pallas kernels, whole(): pl.pallas_call(functools.partial(whole_kernel, n, m), out_shape=[jax.Shap...  65 us
    pallas_call x1, Pallas kernels, hand_out(): pl.pallas_call(hand_out_kernel, out_shape=[jax.ShapeDtypeStruct(x.shape,...  2.07 us

profile of v7, /device:TPU:0, one launch (start us, length us, event | category | flops | bytes accessed | tf_op | source)
XLA Modules:
  0.0 67.7 jit_solution(8944802308246835041)
XLA Ops:
  0.6 65.0 %whole_step.1 = (bf16[128,512]{1,0:T(8,128)(2,1)}, bf16[128,512]{1,0:T(8,128)(2,1)}, bf16[224,128]{1,0:T(8,128)(2,1)}, f32[112,2,512]{2,1,0:T(2,128)}) custom-call(bf16[112,2,512]{2,1,0:T(2,128)(2,1)} %w_ref.1, bf16[128,896]{1,0:T(8,128)(2,1)} %e_ref.1, bf16[128,512]{1,0:T(8,128)(2,1)} %q_ref.1, bf16[128,512]{1,0:T(8,128)(2,1)} %c_ref.1, s32[2,2]{1,0:T(2,128)} %p_ref.1), custom_call_target="tpu_custom_call" | custom-call | tf_op jit(solution)/shard_map/whole_step/pallas_call | solution.py:332
  65.7 2.1 %hand_out.1 = (bf16[128,512]{1,0:T(8,128)(2,1)}, bf16[128,512]{1,0:T(8,128)(2,1)}, bf16[224,128]{1,0:T(8,128)(2,1)}, f32[112,2,512]{2,1,0:T(2,128)}) custom-call(bf16[128,512]{1,0:T(8,128)(2,1)} %get-tuple-element.12.refs_0_, bf16[128,512]{1,0:T(8,128)(2,1)} %get-tuple-element.13.refs_1_, bf16[224,128]{1,0:T(8,128)(2,1)} %get-tuple-element.14.refs_2_, ...), custom_call_target="tpu_custom_call" | custom-call | tf_op jit(solution)/shard_map/hand_out/pallas_call | solution.py:377
